TPU v7x, 128 devices: a whole 4x4x4 slice. The times are simulated.
128 devices in a mesh: sp: 4 (over z_hi, core), tx: 8 (over z_lo, x), ty: 4 (over y).
Axes of the slice: x: 4, y: 4, z: 4 (z_hi: 2, z_lo: 2; z = z_hi * 2 + z_lo), core: 2. Of those that a mesh axis runs over, the one named last changes fastest.
Arguments:
- mass_fractions: float32 [8, 8, 512, 1024], P('sp', None, ('tx', 'ty')), may hold values from 0 to 1
Outputs:
- correlation: float32 [28, 8, 512, 1024], P(None, 'sp', 'tx', 'ty')
All inputs are finite; a program needn't handle non-finite values.
Results may differ from a plain program's by a relative error of at most 0.00013.
Values sent between devices are 32-bit elements; how exact they have to be, the bound alone decides.
A program may use at most 64 MiB of HBM per device.

v0:
```python
import jax
import jax.numpy as jnp
from jax import lax
from jax.sharding import PartitionSpec as P

EPS = 1e-06


def extended(shard, sides, width):
    for axis, dim in sides:
        size, length = (lax.axis_size(axis), shard.shape[dim])
        up = [(i, (i + 1) % size) for i in range(size - 1)]
        down = [(j, i) for i, j in up]
        last = lax.slice_in_dim(shard, length - width, length, axis=dim)
        initial = lax.slice_in_dim(shard, 0, width, axis=dim)
        before = lax.ppermute(last, axis, up)
        after = lax.ppermute(initial, axis, down)
        shard = jnp.concatenate([before, shard, after], axis=dim)
    return shard


def window_sum(padded, which):
    length = padded.shape[which] - 4
    running = lax.slice_in_dim(padded, 0, length, axis=which)
    for offset in range(1, 5):
        running = running + lax.slice_in_dim(padded, offset, offset + length, axis=which)
    return running


def edge_counts(anchor, length_here, extent):
    position = anchor + jnp.arange(length_here, dtype=jnp.int32)
    upper = jnp.minimum(position + 2, extent - 1)
    lower = jnp.maximum(position - 2, 0)
    return (upper - lower + 1).astype(jnp.float32)


def shards(mass_fractions):
    tile_cells = lax.all_to_all(
        lax.all_to_all(mass_fractions, "sp", split_axis=1, concat_axis=0, tiled=True),
        "ty",
        split_axis=3,
        concat_axis=2,
        tiled=True,
    )
    padded = extended(tile_cells, (("sp", 1), ("tx", 2), ("ty", 3)), 2)
    species_count = padded.shape[0]
    depth = padded.shape[1] - 4
    rows_here = padded.shape[2] - 4
    cols_here = padded.shape[3] - 4
    counts = (
        edge_counts(lax.axis_index("sp") * depth, depth, depth * lax.axis_size("sp"))[:, None, None]
        * edge_counts(lax.axis_index("tx") * rows_here, rows_here, rows_here * lax.axis_size("tx"))[
            None, :, None
        ]
        * edge_counts(lax.axis_index("ty") * cols_here, cols_here, cols_here * lax.axis_size("ty"))[
            None, None, :
        ]
    )

    def filtered_product(first_fields, second_fields):
        running = first_fields[:, 0:depth] * second_fields[:, 0:depth]
        for offset in range(1, 5):
            running = (
                running
                + first_fields[:, offset : offset + depth]
                * second_fields[:, offset : offset + depth]
            )
        return window_sum(window_sum(running, 2), 3) / counts

    means = window_sum(window_sum(window_sum(padded, 1), 2), 3) / counts
    variances = filtered_product(padded, padded) - means * means
    pieces = []
    for first in range(species_count - 1):
        single = padded[first : first + 1]
        others = padded[first + 1 :]
        covariance = (
            filtered_product(single, others) - means[first : first + 1] * means[first + 1 :]
        )
        scale = jnp.sqrt((variances[first : first + 1] + EPS) * (variances[first + 1 :] + EPS))
        pieces.append(covariance / scale)
    return jnp.concatenate(pieces, 0)


def solution(mesh):
    return jax.shard_map(
        shards,
        mesh=mesh,
        in_specs=(P("sp", None, ("tx", "ty"), None),),
        out_specs=P(None, "sp", "tx", "ty"),
        check_vma=False,
    )
```

profile of v0, /device:TPU:1, one launch (start us, length us, event | category | flops | bytes accessed | tf_op | source)
XLA Modules:
  0.0 161.6 jit_solution(16154735262456107144)
XLA Ops:
  0.0 1.3 copy.4
  1.3 21.4 %all_to_all.36 = f32[2,8,16,1024]{3,2,0,1:T(8,128)S(1)} all-to-all(f32[2,8,16,1024]{3,2,0,1:T(8,128)S(1)} %copy.4), channel_id=1, replica_groups=mesh['sp'=4,'tx'=8,'ty'=4] {'sp'}, dimensions={1} | all-to-all | bytes 2097152 | tf_op jit(solution)/shard_map/all_to_all | solution.py:39
  22.7 0.1 copy.6
  22.8 8.6 %copy.7 = f32[8,2,16,1024]{2,1,0,3:T(2,128)} copy(f32[8,2,16,1024]{3,2,1,0:T(8,128)S(1)} %bitcast.100) | data formatting | bytes 2097152 | tf_op jit(solution)/shard_map/all_to_all | solution.py:39
  31.4 12.8 %reshape.68 = f32[4,1,65536]{2,1,0:T(1,128)S(1)} reshape(f32[1024,8,2,16]{3,2,1,0:T(2,128)} %bitcast.93) | data formatting | bytes 2097152
  44.3 17.5 %all_to_all.37 = f32[4,1,65536]{2,1,0:T(1,128)S(1)} all-to-all(f32[4,1,65536]{2,1,0:T(1,128)S(1)} %reshape.68), channel_id=1, replica_groups=mesh['sp'=4,'tx'=8,'ty'=4] {'ty'}, dimensions={0} | all-to-all | bytes 2097152 | tf_op jit(solution)/shard_map/all_to_all | solution.py:38
  61.8 0.5 broadcast.166
  62.3 3.7 %reduce = f32[4,65536]{1,0:T(4,128)S(1)} reduce(f32[4,1,65536]{2,1,0:T(1,128)S(1)} %all_to_all.37, f32[]{:T(128)} %broadcast.166), dimensions={1}, to_apply=%all_to_all.30.reduce_sub_computation | reduce | bytes 2097156 | tf_op jit(solution)/shard_map/all_to_all | solution.py:38
  66.0 14.1 %reshape.69 = f32[1024,8,2,16]{3,2,1,0:T(2,128)} reshape(f32[4,65536]{1,0:T(4,128)S(1)} %reduce) | data formatting | bytes 2097152
  80.1 10.5 %copy.15 = f32[8,2,16,4,256]{4,3,2,1,0:T(4,128)S(1)} copy(f32[8,2,16,4,256]{2,1,0,4,3:T(2,128)} %bitcast.94) | data formatting | bytes 2097152 | tf_op jit(solution)/shard_map/all_to_all | solution.py:38
  90.6 0.2 copy.9
  90.8 4.9 %collective-permute-start = (f32[8,2,64,256]{3,2,1,0:T(8,128)S(1)}, f32[8,2,64,256]{3,2,1,0:T(8,128)S(1)}, u32[]{:S(2)}, u32[]{:S(2)}) collective-permute-start(f32[8,2,64,256]{3,2,1,0:T(8,128)S(1)} %bitcast.95), channel_id=1, source_target_pairs={{0,32},{32,64},{64,96},{1,33},{33,65},{65,97},{2,34},{34,66},{66,9... | collective-permute-start | bytes 3145736 | tf_op jit(solution)/shard_map/ppermute | solution.py:16
  95.7 1.9 %collective-permute-start.1 = (f32[8,2,64,256]{3,2,1,0:T(8,128)S(1)}, f32[8,2,64,256]{3,2,1,0:T(8,128)S(1)}, u32[]{:S(2)}, u32[]{:S(2)}) collective-permute-start(f32[8,2,64,256]{3,2,1,0:T(8,128)S(1)} %bitcast.96), channel_id=1, source_target_pairs={{32,0},{64,32},{96,64},{33,1},{65,33},{97,65},{34,2},{66,34},{98,6... | collective-permute-start | bytes 3145736 | tf_op jit(solution)/shard_map/ppermute | solution.py:17
  97.6 0.1 broadcast_multiply_fusion.1
  97.7 10.7 %collective-permute-done = f32[8,2,64,256]{3,2,1,0:T(8,128)S(1)} collective-permute-done((f32[8,2,64,256]{3,2,1,0:T(8,128)S(1)}, f32[8,2,64,256]{3,2,1,0:T(8,128)S(1)}, u32[]{:S(2)}, u32[]{:S(2)}) %collective-permute-start) | collective-permute-done | bytes 1048608 | tf_op jit(solution)/shard_map/ppermute | solution.py:16
  108.5 5.9 %collective-permute-done.1 = f32[8,2,64,256]{3,2,1,0:T(8,128)S(1)} collective-permute-done((f32[8,2,64,256]{3,2,1,0:T(8,128)S(1)}, f32[8,2,64,256]{3,2,1,0:T(8,128)S(1)}, u32[]{:S(2)}, u32[]{:S(2)}) %collective-permute-start.1) | collective-permute-done | bytes 1048608 | tf_op jit(solution)/shard_map/ppermute | solution.py:17
  114.4 0.1 pad_maximum_fusion.4
  114.4 2.1 %collective-permute-start.2 = (f32[8,6,2,256]{3,2,1,0:T(2,128)S(1)}, f32[8,6,2,256]{3,2,1,0:T(2,128)S(1)}, u32[]{:S(2)}, u32[]{:S(2)}) collective-permute-start(f32[8,6,2,256]{3,2,1,0:T(2,128)S(1)} %get-tuple-element.42), channel_id=1, source_target_pairs={{0,4},{4,8},{8,12},{12,16},{16,20},{20,24},{24,28},{1,5},{5,9},{9,... | collective-permute-start | bytes 294920 | tf_op jit(solution)/shard_map/ppermute | solution.py:16
  116.5 1.5 collective-permute-start.3
  118.0 0.1 collective-permute-done.2
  118.1 3.7 %collective-permute-done.3 = f32[8,6,2,256]{3,2,1,0:T(2,128)S(1)} collective-permute-done((f32[8,6,2,256]{3,2,1,0:T(2,128)S(1)}, f32[8,6,2,256]{3,2,1,0:T(2,128)S(1)}, u32[]{:S(2)}, u32[]{:S(2)}) %collective-permute-start.3) | collective-permute-done | bytes 98336 | tf_op jit(solution)/shard_map/ppermute | solution.py:17
  121.9 0.5 pad_maximum_fusion.1
  122.3 2.4 %fusion.80 = (f32[8,6,68,2]{3,2,1,0:T(8,128)}, f32[8,6,68,2]{3,2,1,0:T(8,128)}) fusion(f32[8,6,68,256]{3,2,1,0:T(8,128)S(1)} %pad_maximum_fusion.1), kind=kLoop, calls=%fused_computation.255 | loop fusion | bytes 104448 | tf_op jit(solution)/shard_map/slice | solution.py:14
  124.7 2.1 %copy.10 = f32[8,6,68,2]{2,0,3,1:T(8,128)S(1)} copy(f32[8,6,68,2]{3,2,1,0:T(8,128)} %get-tuple-element.40) | data formatting | bytes 52224 | tf_op jit(solution)/shard_map/slice | solution.py:14
  126.8 2.8 %collective-permute-start.4 = (f32[8,6,68,2]{2,0,3,1:T(8,128)S(1)}, f32[8,6,68,2]{2,0,3,1:T(8,128)}, u32[]{:S(2)}, u32[]{:S(2)}) collective-permute-start(f32[8,6,68,2]{2,0,3,1:T(8,128)S(1)} %copy.10), channel_id=1, source_target_pairs={{0,1},{1,2},{2,3},{4,5},{5,6},{6,7},{8,9},{9,10},{10,11},{12,13},{... | collective-permute-start | bytes 78344 | tf_op jit(solution)/shard_map/ppermute | solution.py:16
  129.6 2.7 %copy.11 = f32[8,6,68,2]{2,0,3,1:T(8,128)} copy(f32[8,6,68,2]{3,2,1,0:T(8,128)} %get-tuple-element.41) | data formatting | bytes 52224 | tf_op jit(solution)/shard_map/slice | solution.py:15
  132.3 1.3 collective-permute-start.5
  133.6 0.1 broadcast_multiply_fusion
  133.7 0.0 collective-permute-done.4
  133.7 2.7 %copy.12 = f32[8,6,68,2]{3,2,1,0:T(8,128)} copy(f32[8,6,68,2]{2,0,3,1:T(8,128)} %collective-permute-done.4) | data formatting | bytes 52224 | tf_op jit(solution)/shard_map/ppermute | solution.py:16
  136.4 1.1 collective-permute-done.5
  137.5 2.7 %copy.13 = f32[8,6,68,2]{3,2,1,0:T(8,128)} copy(f32[8,6,68,2]{2,0,3,1:T(8,128)} %collective-permute-done.5) | data formatting | bytes 52224 | tf_op jit(solution)/shard_map/ppermute | solution.py:17
  140.1 5.6 %pad_maximum_fusion = f32[8,6,68,260]{3,2,1,0:T(8,128)S(1)} fusion(f32[8,6,68,2]{3,2,1,0:T(8,128)} %copy.13, f32[8,6,2,256]{3,2,1,0:T(2,128)S(1)} %collective-permute-done.3, f32[8,2,64,256]{3,2,1,0:T(8,128)S(1)} %collective-permute-done.1, f32[8,2,64,256]{3,2,1,0:T(8,128)S(1)} %bitcast.99, f32[8,2,64,256]{3,2,1,0:T(8,128)S(1)} %collective-permute-done, ...), kind=kLoop, calls=%fused_computation | loop fusion | flops 5091840 | bytes 6789120 | tf_op jit(solution)/shard_map/concatenate | solution.py:18
  145.7 0.3 slice_bitcast_fusion.4
  146.0 0.2 fusion.63
  146.2 0.7 add_add_fusion
  146.9 0.2 fusion.47
  147.1 0.2 slice_add_fusion.56
  147.2 0.2 fusion.31
  147.5 0.2 slice_add_fusion.47
  147.7 0.3 fusion.21
  148.0 0.3 slice_add_fusion.33
  148.3 0.3 fusion.8
  148.7 0.4 slice_add_fusion.24
  149.1 0.4 fusion.4
  149.5 0.5 slice_add_fusion.12
  150.0 0.5 fusion
  150.5 0.5 slice_add_fusion.8
  151.0 1.2 slice_add_fusion
  152.2 2.2 %fusion.13 = (f32[8,2,64,256]{3,2,1,0:T(8,128)S(1)}, f32[8,2,64,256]{3,2,1,0:T(8,128)S(1)}) fusion(f32[8,2,64,260]{3,2,1,0:T(8,128)S(1)} %get-tuple-element.56, f32[2,64,256]{2,1,0:T(8,128)S(1)} %broadcast_multiply_fusion, f32[8,2,64,260]{3,2,1,0:T(8,128)S(1)} %get-tuple-element.57), kind=kLoop, calls=%fused_computation.49 | loop fusion | flops 3145728 | bytes 12713984 | tf_op jit(solution)/shard_map/sub | solution.py:71
  154.5 0.1 slice_bitcast_fusion.30
  154.5 0.1 fusion.73
  154.6 0.1 slice_add_fusion.70
  154.7 1.0 fusion.18
  155.7 0.9 fusion.28
  156.7 0.8 fusion.38
  157.4 0.6 fusion.44
  158.1 0.5 fusion.54
  158.6 0.3 fusion.60
  158.9 0.0 copy-start
  158.9 1.8 %copy-done = f32[28,2,64,256]{3,2,1,0:T(8,128)} copy-done((f32[28,2,64,256]{3,2,1,0:T(8,128)}, f32[28,2,64,256]{3,2,1,0:T(8,128)S(1)}, u32[]{:S(2)}) %copy-start) | copy-done | bytes 3670040
  160.7 0.9 fusion.70
  (4 shorter events, 0.1 us)
Async XLA Ops:
  90.8 17.7 %collective-permute-start = (f32[8,2,64,256]{3,2,1,0:T(8,128)S(1)}, f32[8,2,64,256]{3,2,1,0:T(8,128)S(1)}, u32[]{:S(2)}, u32[]{:S(2)}) collective-permute-start(f32[8,2,64,256]{3,2,1,0:T(8,128)S(1)} %bitcast.95), channel_id=1, source_target_pairs={{0,32},{32,64},{64,96},{1,33},{33,65},{65,97},{2,34},{34,66},{66,9... | collective-permute-start | bytes 3145736 | tf_op jit(solution)/shard_map/ppermute | solution.py:16
  95.7 18.7 %collective-permute-start.1 = (f32[8,2,64,256]{3,2,1,0:T(8,128)S(1)}, f32[8,2,64,256]{3,2,1,0:T(8,128)S(1)}, u32[]{:S(2)}, u32[]{:S(2)}) collective-permute-start(f32[8,2,64,256]{3,2,1,0:T(8,128)S(1)} %bitcast.96), channel_id=1, source_target_pairs={{32,0},{64,32},{96,64},{33,1},{65,33},{97,65},{34,2},{66,34},{98,6... | collective-permute-start | bytes 3145736 | tf_op jit(solution)/shard_map/ppermute | solution.py:17
  114.4 3.7 %collective-permute-start.2 = (f32[8,6,2,256]{3,2,1,0:T(2,128)S(1)}, f32[8,6,2,256]{3,2,1,0:T(2,128)S(1)}, u32[]{:S(2)}, u32[]{:S(2)}) collective-permute-start(f32[8,6,2,256]{3,2,1,0:T(2,128)S(1)} %get-tuple-element.42), channel_id=1, source_target_pairs={{0,4},{4,8},{8,12},{12,16},{16,20},{20,24},{24,28},{1,5},{5,9},{9,... | collective-permute-start | bytes 294920 | tf_op jit(solution)/shard_map/ppermute | solution.py:16
  116.5 5.4 %collective-permute-start.3 = (f32[8,6,2,256]{3,2,1,0:T(2,128)S(1)}, f32[8,6,2,256]{3,2,1,0:T(2,128)S(1)}, u32[]{:S(2)}, u32[]{:S(2)}) collective-permute-start(f32[8,6,2,256]{3,2,1,0:T(2,128)S(1)} %get-tuple-element.43), channel_id=1, source_target_pairs={{4,0},{8,4},{12,8},{16,12},{20,16},{24,20},{28,24},{5,1},{9,5},{13... | collective-permute-start | bytes 294920 | tf_op jit(solution)/shard_map/ppermute | solution.py:17
  126.8 6.9 %collective-permute-start.4 = (f32[8,6,68,2]{2,0,3,1:T(8,128)S(1)}, f32[8,6,68,2]{2,0,3,1:T(8,128)}, u32[]{:S(2)}, u32[]{:S(2)}) collective-permute-start(f32[8,6,68,2]{2,0,3,1:T(8,128)S(1)} %copy.10), channel_id=1, source_target_pairs={{0,1},{1,2},{2,3},{4,5},{5,6},{6,7},{8,9},{9,10},{10,11},{12,13},{... | collective-permute-start | bytes 78344 | tf_op jit(solution)/shard_map/ppermute | solution.py:16
  132.3 5.1 %collective-permute-start.5 = (f32[8,6,68,2]{2,0,3,1:T(8,128)}, f32[8,6,68,2]{2,0,3,1:T(8,128)}, u32[]{:S(2)}, u32[]{:S(2)}) collective-permute-start(f32[8,6,68,2]{2,0,3,1:T(8,128)} %copy.11), channel_id=1, source_target_pairs={{1,0},{2,1},{3,2},{5,4},{6,5},{7,6},{9,8},{10,9},{11,10},{13,12},{... | collective-permute-start | bytes 78344 | tf_op jit(solution)/shard_map/ppermute | solution.py:17
  158.9 1.8 %copy-start = (f32[28,2,64,256]{3,2,1,0:T(8,128)}, f32[28,2,64,256]{3,2,1,0:T(8,128)S(1)}, u32[]{:S(2)}) copy-start(f32[28,2,64,256]{3,2,1,0:T(8,128)S(1)} %fusion.60) | copy-start | bytes 11010052
where the time goes:
time: 163 us; the launch traced here: 162 us
  local copies, waits for them, and re-layouts  62.9 us (39%)
  blocking collectives  38.9 us (24%)
  other arithmetic  23.5 us (14%)
  waiting for transfers between devices  21.5 us (13%)
  starting transfers between devices  14.5 us (9%)
    unnamed x5, local copies, waits for them, and re-layouts  30.1 us
    all_to_all x1, blocking collectives, shards(): lax.all_to_all(mass_fractions, 'sp', split_axis=1, concat_axis=0, tiled=T...  21.4 us
    all_to_all x1, blocking collectives, shards(): lax.all_to_all(lax.all_to_all(mass_fractions, 'sp', split_axis=1, concat_...  17.5 us
    all_to_all x3, local copies, waits for them, and re-layouts, shards(): lax.all_to_all(lax.all_to_all(mass_fractions, 'sp', split_axis=1, concat_...  11.2 us
    ppermute x3, waiting for transfers between devices, extended(): before = lax.ppermute(last, axis, up)  10.8 us
    ppermute x3, waiting for transfers between devices, extended(): after = lax.ppermute(initial, axis, down)  10.7 us
    ppermute x3, starting transfers between devices, extended(): before = lax.ppermute(last, axis, up)  9.76 us
    all_to_all x2, local copies, waits for them, and re-layouts, shards(): lax.all_to_all(mass_fractions, 'sp', split_axis=1, concat_axis=0, tiled=T...  8.72 us
  transfers between devices with their start and end apart: 6, of which 5 were waited for; matrix products, arithmetic and copies ran while one was open for 3% of the time, Pallas kernels for 0%

commit v1 on v0

v1 whole, which is shorter than its diff:
```python
import functools

import jax
import jax.numpy as jnp
from jax import lax
from jax.experimental import pallas as pl
from jax.experimental.pallas import tpu as pltpu
from jax.sharding import PartitionSpec as P

EPS = 1e-06
MESH = pl.DeviceIdType.MESH
S, NZ, NX, NY = 8, 8, 512, 1024
ROWS, COLS, BLK = 64, 256, 16
PAIRS = [(i, j) for i in range(S) for j in range(i + 1, S)]
FIELDS = [(i, None) for i in range(S)] + [(i, i) for i in range(S)] + PAIRS
NF = len(FIELDS)
ORDER = (1, 3, 2)


def kernel(
    x_hbm, o_hbm, xin, m, yh, yhb, xb, yhs, xhs, zs, zh, ov,
    ysend, yrecv, zsend, zrecv, csend, crecv, lsem, osem,
):
    sp, tx, ty = (lax.axis_index(a) for a in ("sp", "tx", "ty"))
    zhi = lax.div(sp, 2)
    core = lax.rem(sp, 2)
    zsp = lax.rem(sp + 2, 4)
    csp = sp + 1 - 2 * core
    p_here = 2 * zhi
    p_there = 2 - 2 * zhi

    barrier = pltpu.get_barrier_semaphore()

    def greet(dev):
        pl.semaphore_signal(barrier, inc=1, device_id=dev, device_id_type=MESH)

    for k in (1, 2, 3):
        greet((sp, tx, lax.rem(ty + k, 4)))
    greet((zsp, tx, ty))
    greet((csp, tx, ty))

    @pl.when(tx > 0)
    def _():
        greet((sp, tx - 1, 3))

    @pl.when(tx < 7)
    def _():
        greet((sp, tx + 1, 0))

    up = jnp.logical_and(ty == 3, tx < 7)
    down = jnp.logical_and(ty == 0, tx > 0)
    load = pltpu.make_async_copy(x_hbm, xin, lsem.at[0])
    load.start()

    for s in range(S):
        m[s, 0:2] = jnp.zeros((2, 72, COLS), jnp.float32)
        m[s, 10:12] = jnp.zeros((2, 72, COLS), jnp.float32)

    @pl.when(tx == 0)
    def _():
        xb[sp, 0] = jnp.zeros((32, COLS), jnp.float32)
        yhb[sp, 0] = jnp.zeros((8, 128), jnp.float32)

    @pl.when(tx == 7)
    def _():
        xb[sp, 1] = jnp.zeros((32, COLS), jnp.float32)
        yhb[sp, 1] = jnp.zeros((8, 128), jnp.float32)

    load.wait()
    pl.semaphore_wait(barrier, 5 + 4 * up.astype(jnp.int32) + 4 * down.astype(jnp.int32))

    def rcopy(src, dst, ss, rs, dev):
        return pltpu.make_async_remote_copy(
            src_ref=src, dst_ref=dst, send_sem=ss, recv_sem=rs, device_id=dev, device_id_type=MESH
        )

    def cols(y):
        return pl.ds(pl.multiple_of(y * COLS, COLS), COLS)

    def rows(b):
        return pl.ds(pl.multiple_of(b * BLK, BLK), BLK)

    mine = pl.ds(2 * sp, 2)
    far = pl.ds(2 * zsp, 2)
    zdev = (zsp, tx, ty)
    cdev = (csp, tx, ty)
    six = pl.ds(p_here + 2, 6)
    six_there = pl.ds(p_there + 2, 6)

    def zcopy(q, b, first=False):
        src = xin.at[:, pl.ds(p_there, 6), :, cols(ty)] if first else m.at[mine, six_there, rows(b)]
        return rcopy(src, m.at[mine, six_there, rows(b)], zsend.at[q], zrecv.at[q], zdev)

    def ccopy(q, who, b, first=False):
        src = xin.at[:, pl.ds(p_here, 6), :, cols(ty)] if first else m.at[who, six, rows(b)]
        return rcopy(src, m.at[who, six, rows(b)], csend.at[q], crecv.at[q], cdev)

    sent = []

    def go(c):
        c.start()
        sent.append(c)

    go(zcopy(0, ty, True))
    ycopies = {}
    for k in ORDER:
        y = lax.rem(ty + k, 4)
        ycopies[k] = rcopy(
            xin.at[:, :, :, cols(y)], m.at[mine, pl.ds(2, 8), rows(ty)], ysend.at[k], yrecv.at[k], (sp, tx, y)
        )
        go(ycopies[k])
    go(ccopy(0, mine, ty, True))
    own = pltpu.make_async_copy(xin.at[:, :, :, cols(ty)], m.at[mine, pl.ds(2, 8), rows(ty)], lsem.at[1])
    own.start()

    lane = lax.broadcasted_iota(jnp.int32, (BLK, 128), 1)
    for y in range(4):
        acc = jnp.zeros((BLK, 128), jnp.float32)
        for s in range(2):
            for z in range(NZ):
                base = 48 * s + 4 * (z + 2)
                zero = jnp.zeros((BLK, 128), jnp.float32)
                left = xin[s, z, :, y * COLS - 128 : y * COLS] if y > 0 else zero
                right = xin[s, z, :, y * COLS + COLS : y * COLS + COLS + 128] if y < 3 else zero
                both = pltpu.roll(jnp.where(lane >= 64, left, right), base + 2, 1)
                acc = jnp.where(jnp.logical_and(lane >= base, lane < base + 4), both, acc)
        yhs[y] = acc
    for k in ORDER:
        y = lax.rem(ty + k, 4)
        c = rcopy(yhs.at[y], yh.at[sp, rows(ty)], ysend.at[4 + k], yrecv.at[4 + k], (sp, tx, y))
        ycopies[4 + k] = c
        go(c)
    ownh = pltpu.make_async_copy(yhs.at[ty], yh.at[sp, rows(ty)], lsem.at[2])
    ownh.start()

    def pack_rows(first):
        for z in range(NZ):
            for s in range(2):
                xhs[4 * z + 2 * s : 4 * z + 2 * s + 2, :] = xin[s, z, first : first + 2, :]

    def xcopies(side, y):
        dev = (sp, tx + 1 if side == 0 else tx - 1, y)
        half = 8 if side == 0 else 0
        q = 8 + 4 * side + y
        return (
            rcopy(xhs.at[:, y * COLS : (y + 1) * COLS], xb.at[sp, side], ysend.at[q], yrecv.at[8 + side], dev),
            rcopy(yhs.at[y, half : half + 8], yhb.at[sp, side], ysend.at[8 + q], yrecv.at[10 + side], dev),
        )

    for side, cond, first in ((0, up, 14), (1, down, 0)):

        @pl.when(cond)
        def _(side=side, first=first):
            pack_rows(first)
            for y in range(4):
                for c in xcopies(side, y):
                    c.start()

    own.wait()
    ownh.wait()

    def zhcopy(q, b):
        return rcopy(yh.at[sp, rows(b)], yh.at[sp, rows(b)], zsend.at[q], zrecv.at[q], zdev)

    def chcopy(q, who, b):
        return rcopy(yh.at[who, rows(b)], yh.at[who, rows(b)], csend.at[q], crecv.at[q], cdev)

    go(zhcopy(4, ty))
    go(chcopy(4, sp, ty))
    for n, k in enumerate(ORDER):
        b = lax.rem(ty + 4 - k, 4)
        ycopies[k].wait_recv()
        go(zcopy(1 + n, b))
        go(ccopy(1 + n, mine, b))
        ycopies[4 + k].wait_recv()
        go(zhcopy(5 + n, b))
        go(chcopy(5 + n, sp, b))

    @pl.when(tx > 0)
    def _():
        for c in xcopies(0, 0):
            c.wait_recv()

    @pl.when(tx < 7)
    def _():
        for c in xcopies(1, 0):
            c.wait_recv()

    def xrows(first):
        return pl.ds(pl.multiple_of(first * 4, 8), 24)

    z_x = rcopy(xb.at[sp, :, xrows(p_there)], xb.at[sp, :, xrows(p_there)], zsend.at[8], zrecv.at[8], zdev)
    z_yb = rcopy(yhb.at[sp], yhb.at[sp], zsend.at[9], zrecv.at[9], zdev)
    go(z_x)
    go(z_yb)

    def cx(q, who):
        return rcopy(xb.at[who, :, xrows(p_here)], xb.at[who, :, xrows(p_here)], csend.at[q], crecv.at[q], cdev)

    def cyb(q, who):
        return rcopy(yhb.at[who], yhb.at[who], csend.at[q], crecv.at[q], cdev)

    go(cx(8, sp))
    go(cyb(9, sp))

    for n, k in enumerate((0,) + ORDER):
        b = lax.rem(ty + 4 - k, 4)
        zcopy(n, b).wait_recv()
        go(ccopy(10 + n, far, b))
        zhcopy(4 + n, b).wait_recv()
        go(chcopy(14 + n, zsp, b))
    z_x.wait_recv()
    go(cx(18, zsp))
    z_yb.wait_recv()
    go(cyb(19, zsp))
    for q in range(4):
        b = ty
        ccopy(q, mine, b).wait_recv()
        chcopy(4 + q, sp, b).wait_recv()
        ccopy(10 + q, mine, b).wait_recv()
        chcopy(14 + q, sp, b).wait_recv()
    for q in (8, 18):
        cx(q, sp).wait_recv()
        cyb(q + 1, sp).wait_recv()

    for i in range(S):
        for z in range(NZ):
            r = 4 * z + 2 * (i % 2)
            m[i, 2 + z, 64:66, :] = xb[i // 2, 1, r : r + 2, :]
            m[i, 2 + z, 70:72, :] = xb[i // 2, 0, r : r + 2, :]
    row8 = lax.broadcasted_iota(jnp.int32, (8, 128), 0)
    for q in range(4):
        yh[q, 64:72] = jnp.where(row8 < 4, yhb[q, 1], yhb[q, 0])

    def put(f, p, ct, rt, v):
        zs[2 * f + p, ct, pl.ds(pl.multiple_of(rt * 8 + 8, 8), 8), :] = v

        @pl.when(rt == 8)
        def _():
            zs[2 * f + p, ct, 0:8, :] = v

    def stage1(rt, _):
        tile = pl.ds(pl.multiple_of(rt * 8, 8), 8)
        for ct in range(2):
            v = [[m[i, 2 * sp + k, tile, ct * 128 : ct * 128 + 128] for k in range(6)] for i in range(S)]
            for f, (i, j) in enumerate(FIELDS):
                p = v[i] if j is None else [a * b for a, b in zip(v[i], v[j])]
                mid = (p[1] + p[2]) + (p[3] + p[4])
                zs[2 * f, ct, pl.ds(pl.multiple_of(rt * 8 + 8, 8), 8), :] = p[0] + mid
                zs[2 * f + 1, ct, pl.ds(pl.multiple_of(rt * 8 + 8, 8), 8), :] = mid + p[5]
        h = [
            pltpu.roll(yh[i // 2, tile, :], lax.rem(256 - 48 * (i % 2) - 8 * sp, 128), 1) for i in range(S)
        ]
        for f, (i, j) in enumerate(FIELDS):
            p = h[i] if j is None else h[i] * h[j]
            p1 = p + pltpu.roll(p, 124, 1)
            p2 = p1 + pltpu.roll(p1, 120, 1)
            zh[f, pl.ds(pl.multiple_of(rt * 8 + 8, 8), 8), :] = p2 + pltpu.roll(p, 112, 1)
        return 0

    lax.fori_loop(0, 9, stage1, 0)

    def wrap(f, _):
        zs[2 * f, :, 0:8, :] = zs[2 * f, :, 72:80, :]
        zs[2 * f + 1, :, 0:8, :] = zs[2 * f + 1, :, 72:80, :]
        zh[f, 0:8, :] = zh[f, 72:80, :]
        return 0

    lax.fori_loop(0, NF, wrap, 0)

    lane8 = lax.broadcasted_iota(jnp.int32, (8, 128), 1)
    lt127, ge2, lt126 = lane8 < 127, lane8 >= 2, lane8 < 126

    def span(pos, extent):
        return (jnp.minimum(pos + 2, extent - 1) - jnp.maximum(pos - 2, 0) + 1).astype(jnp.float32)

    def xsum(ref, x0):
        w = [ref[pl.ds(x0 * 8 + 6 + k, 8), :] for k in range(5)]
        return ((w[0] + w[1]) + (w[2] + w[3])) + w[4]

    def stage2(x0, _):
        out_rows = pl.ds(pl.multiple_of(x0 * 8, 8), 8)
        cx_ = span(tx * ROWS + x0 * 8 + row8, NX)
        for p in range(2):
            cz = span(2 * sp + p, NZ)
            inv = [1.0 / (cx_ * span(ty * COLS + ct * 128 + lane8, NY) * cz) for ct in range(2)]

            def box(f):
                t0, t1 = (xsum(zs.at[2 * f + p, ct], x0) for ct in range(2))
                h = pltpu.roll(xsum(zh.at[f], x0), 126 - 4 * p, 1)
                r0, r1, rh = (pltpu.roll(t, 127, 1) for t in (t0, t1, h))
                a0 = t0 + jnp.where(lt127, r0, r1)
                a1 = t1 + jnp.where(lt127, r1, rh)
                ah = h + jnp.where(lt127, rh, r0)
                r0, r1, rh = (pltpu.roll(t, 2, 1) for t in (a0, a1, ah))
                b0 = a0 + jnp.where(ge2, r0, rh)
                b1 = a1 + jnp.where(ge2, r1, r0)
                r0, r1, rh = (pltpu.roll(t, 126, 1) for t in (t0, t1, h))
                return (
                    (b0 + jnp.where(lt126, r0, r1)) * inv[0],
                    (b1 + jnp.where(lt126, r1, rh)) * inv[1],
                )

            means = [box(i) for i in range(S)]
            var = []
            for i in range(S):
                sq = box(S + i)
                var.append(tuple(sq[t] - means[i][t] * means[i][t] + EPS for t in range(2)))
            for n, (i, j) in enumerate(PAIRS):
                pr = box(2 * S + n)
                for t in range(2):
                    cov = pr[t] - means[i][t] * means[j][t]
                    ov[n, p, out_rows, t * 128 : t * 128 + 128] = cov * lax.rsqrt(var[i][t] * var[j][t])
        pltpu.make_async_copy(ov.at[:, :, out_rows], o_hbm.at[:, :, out_rows], osem).start()
        return 0

    lax.fori_loop(0, 8, stage2, 0)
    pltpu.make_async_copy(ov, o_hbm, osem).wait()

    for c in sent:
        c.wait_send()
    for side, cond in ((0, up), (1, down)):

        @pl.when(cond)
        def _(side=side):
            for y in range(4):
                for c in xcopies(side, y):
                    c.wait_send()


def shards(x):
    f32 = jnp.float32
    return pl.pallas_call(
        kernel,
        out_shape=jax.ShapeDtypeStruct((len(PAIRS), 2, ROWS, COLS), f32),
        in_specs=[pl.BlockSpec(memory_space=pl.ANY)],
        out_specs=pl.BlockSpec(memory_space=pl.ANY),
        scratch_shapes=[
            pltpu.VMEM((2, NZ, BLK, NY), f32),
            pltpu.VMEM((S, 12, 72, COLS), f32),
            pltpu.VMEM((4, 72, 128), f32),
            pltpu.VMEM((4, 2, 8, 128), f32),
            pltpu.VMEM((4, 2, 32, COLS), f32),
            pltpu.VMEM((4, BLK, 128), f32),
            pltpu.VMEM((32, NY), f32),
            pltpu.VMEM((2 * NF, 2, 80, 128), f32),
            pltpu.VMEM((NF, 80, 128), f32),
            pltpu.VMEM((len(PAIRS), 2, ROWS, COLS), f32),
            pltpu.SemaphoreType.DMA((24,)),
            pltpu.SemaphoreType.DMA((12,)),
            pltpu.SemaphoreType.DMA((10,)),
            pltpu.SemaphoreType.DMA((10,)),
            pltpu.SemaphoreType.DMA((20,)),
            pltpu.SemaphoreType.DMA((20,)),
            pltpu.SemaphoreType.DMA((3,)),
            pltpu.SemaphoreType.DMA,
        ],
        name="correlate",
        compiler_params=pltpu.CompilerParams(
            collective_id=0, has_side_effects=True, vmem_limit_bytes=48 << 20
        ),
    )(x)


def solution(mesh):
    return jax.shard_map(
        shards,
        mesh=mesh,
        in_specs=(P("sp", None, ("tx", "ty"), None),),
        out_specs=P(None, "sp", "tx", "ty"),
        check_vma=False,
    )
```

time: 163 us -> 125 us (0.77)
  Pallas kernels: 0 us -> 122 us
  local copies, waits for them, and re-layouts: 62.9 us -> 3.06 us
  blocking collectives: 38.9 us -> 0 us
  other arithmetic: 23.5 us -> 0 us
  waiting for transfers between devices: 21.5 us -> 0 us
  starting transfers between devices: 14.5 us -> 0 us
    pallas_call x0 -> x1, Pallas kernels: none -> 122 us  [shards(): pl.pallas_call(kernel, out_shape=jax.ShapeDtypeStruct((len(PAIRS), 2, ROW...]
    all_to_all x2 -> x0, blocking collectives: 38.9 us -> none  [the longest x1 21.4 us: shards(): lax.all_to_all(mass_fractions, 'sp', split_axis=1, concat_axis=0, tiled=T...]
    unnamed x5 -> x3, local copies, waits for them, and re-layouts: 30.1 us -> 3.06 us
    ppermute x6 -> x0, waiting for transfers between devices: 21.5 us -> none  [the longest x3 10.8 us: extended(): before = lax.ppermute(last, axis, up)]
    all_to_all x5 -> x0, local copies, waits for them, and re-layouts: 19.9 us -> none  [the longest x3 11.2 us: shards(): lax.all_to_all(lax.all_to_all(mass_fractions, 'sp', split_axis=1, concat_...]
    ppermute x6 -> x0, starting transfers between devices: 14.5 us -> none  [the longest x3 9.76 us: extended(): before = lax.ppermute(last, axis, up)]
    slice x3 -> x0, local copies, waits for them, and re-layouts: 7.16 us -> none  [the longest x2 4.44 us: extended(): last = lax.slice_in_dim(shard, length - width, length, axis=dim)]
    concatenate x3 -> x0, other arithmetic: 6.95 us -> none  [the longest x2 6.07 us: extended(): shard = jnp.concatenate([before, shard, after], axis=dim)]
  transfers between devices with their start and end apart: 6 -> 0, of which waited for: 5 -> 0; matrix products, arithmetic and copies ran while one was open for 3% -> 0% of each run, Pallas kernels for 0% -> 0%
where the time goes in v1:
time: 125 us
  Pallas kernels  122 us (98%)
  local copies, waits for them, and re-layouts  3.06 us (2%)
    pallas_call x1, Pallas kernels, shards(): pl.pallas_call(kernel, out_shape=jax.ShapeDtypeStruct((len(PAIRS), 2, ROW...  122 us
    unnamed x3, local copies, waits for them, and re-layouts  3.06 us

profile of v1, /device:TPU:1, one launch (start us, length us, event | category | flops | bytes accessed | tf_op | source)
XLA Modules:
  0.0 125.1 jit_solution(14823077777530049384)
XLA Ops:
  0.0 0.0 copy-start
  0.0 1.2 copy-done
  1.2 122.0 %correlate.1 = f32[28,2,64,256]{3,2,1,0:T(8,128)S(1)} custom-call(f32[2,8,16,1024]{3,2,1,0:T(8,128)S(1)} %copy-done), custom_call_target="tpu_custom_call" | custom-call | tf_op jit(solution)/shard_map/correlate/pallas_call | solution.py:333
  123.3 1.8 %copy.3 = f32[28,2,64,256]{3,2,1,0:T(8,128)} copy(f32[28,2,64,256]{3,2,1,0:T(8,128)S(1)} %correlate.1) | data formatting | bytes 7340032
Async XLA Ops:
  0.0 1.2 copy-start

commit v2 on v1

v2 whole, which is shorter than its diff:
```python
import functools

import jax
import jax.numpy as jnp
from jax import lax
from jax.experimental import pallas as pl
from jax.experimental.pallas import tpu as pltpu
from jax.sharding import PartitionSpec as P

EPS = 1e-06
MESH = pl.DeviceIdType.MESH
S, NZ, NX, NY = 8, 8, 512, 1024
ROWS, COLS, BLK = 64, 256, 16
PAIRS = [(i, j) for i in range(S) for j in range(i + 1, S)]
FIELDS = [(i, None) for i in range(S)] + [(i, i) for i in range(S)] + PAIRS
NF = len(FIELDS)
ORDER = (2, 1, 3)


def kernel(
    xin, o_ref, m, stage, yh, yhb, xb, yhs, xhs, zs, zh, xs, ys, band,
    zsend, zrecv, ysend, yrecv, fsend, frecv, csend, crecv, hsend, hrecv, xsend, xrecv, lsem,
):
    sp, tx, ty = (lax.axis_index(a) for a in ("sp", "tx", "ty"))
    zhi = lax.div(sp, 2)
    core = lax.rem(sp, 2)
    zsp = lax.rem(sp + 2, 4)
    csp = sp + 1 - 2 * core
    p_here = 2 * zhi
    p_there = 2 - 2 * zhi
    after = [lax.rem(ty + k, 4) for k in range(4)]
    before = [lax.rem(ty + 4 - k, 4) for k in range(4)]
    up = jnp.logical_and(ty == 3, tx < 7)
    down = jnp.logical_and(ty == 0, tx > 0)

    barrier = pltpu.get_barrier_semaphore()

    def greet(*dev):
        pl.semaphore_signal(barrier, inc=1, device_id=dev, device_id_type=MESH)

    greet(zsp, tx, ty)
    greet(csp, tx, ty)
    for k in (1, 2, 3):
        greet(sp, tx, after[k])
        greet(zsp, tx, after[k])

    @pl.when(tx > 0)
    def _():
        greet(sp, tx - 1, 3)
        greet(zsp, tx - 1, 3)

    @pl.when(tx < 7)
    def _():
        greet(sp, tx + 1, 0)
        greet(zsp, tx + 1, 0)


    for s in range(S):
        m[s, 0:2] = jnp.zeros((2, 72, COLS), jnp.float32)
        m[s, 10:12] = jnp.zeros((2, 72, COLS), jnp.float32)

    @pl.when(tx == 0)
    def _():
        xb[sp, 0] = jnp.zeros((32, COLS), jnp.float32)
        for q in (sp, zsp):
            yhb[q, 0] = jnp.zeros((8, 128), jnp.float32)

    @pl.when(tx == 7)
    def _():
        xb[sp, 1] = jnp.zeros((32, COLS), jnp.float32)
        for q in (sp, zsp):
            yhb[q, 1] = jnp.zeros((8, 128), jnp.float32)

    r_at = lax.broadcasted_iota(jnp.int32, (COLS, COLS), 0)
    c_at = lax.broadcasted_iota(jnp.int32, (COLS, COLS), 1)
    band[...] = jnp.where(jnp.abs(r_at - c_at) <= 2, 1.0, 0.0).astype(jnp.bfloat16)

    pl.semaphore_wait(barrier, 8 + 8 * up.astype(jnp.int32) + 8 * down.astype(jnp.int32))

    def rcopy(src, dst, ss, rs, dev):
        return pltpu.make_async_remote_copy(
            src_ref=src, dst_ref=dst, send_sem=ss, recv_sem=rs, device_id=dev, device_id_type=MESH
        )

    def cols(y):
        return pl.ds(pl.multiple_of(y * COLS, COLS), COLS)

    def rows(b):
        return pl.ds(pl.multiple_of(b * BLK, BLK), BLK)

    zdev = (zsp, tx, ty)
    cdev = (csp, tx, ty)
    six = pl.ds(p_here + 2, 6)
    six_there = pl.ds(p_there + 2, 6)
    sent = []

    def go(c):
        c.start()
        sent.append(c)

    def zcopy(k, s):
        src = xin.at[s, pl.ds(p_there, 6), :, cols(after[k])]
        dst = stage.at[k - 1, s] if k else m.at[2 * sp + s, six_there, rows(ty)]
        return rcopy(src, dst, zsend.at[2 * k + s], zrecv.at[2 * k + s], zdev)

    def ycopy(k):
        return rcopy(
            xin.at[:, pl.ds(p_here, 6), :, cols(after[k])],
            m.at[pl.ds(2 * sp, 2), six, rows(ty)], ysend.at[k], yrecv.at[k], (sp, tx, after[k]),
        )

    def fcopy(k, s):
        return rcopy(
            stage.at[k - 1, s], m.at[2 * zsp + s, six, rows(ty)],
            fsend.at[2 * k + s], frecv.at[2 * k + s], (sp, tx, after[k]),
        )

    def ccopy(k):
        if k == 0:
            src = xin.at[:, pl.ds(p_here, 6), :, cols(ty)]
        else:
            src = m.at[pl.ds(2 * sp, 2), six, rows(before[k])]
        return rcopy(
            src, m.at[pl.ds(2 * sp, 2), six, rows(before[k])], csend.at[k], crecv.at[k], cdev
        )

    def cfcopy(k, s):
        ref = m.at[2 * zsp + s, six, rows(before[k])]
        return rcopy(ref, ref, csend.at[4 + 2 * k + s], crecv.at[4 + 2 * k + s], cdev)

    PIECES = ((2, 0), (2, 1), (1, 0), (3, 0), (1, 1), (3, 1), (0, 0), (0, 1))
    for k, s in PIECES:
        go(zcopy(k, s))
    for k in ORDER:
        go(ycopy(k))
    go(ccopy(0))
    own = pltpu.make_async_copy(
        xin.at[:, pl.ds(p_here, 6), :, cols(ty)], m.at[pl.ds(2 * sp, 2), six, rows(ty)], lsem.at[1]
    )
    own.start()

    lane = lax.broadcasted_iota(jnp.int32, (BLK, 128), 1)
    for y in range(4):
        acc = jnp.zeros((BLK, 128), jnp.float32)
        for s in range(2):
            for z in range(NZ):
                base = 48 * s + 4 * (z + 2)
                zero = jnp.zeros((BLK, 128), jnp.float32)
                left = xin[s, z, :, y * COLS - 128 : y * COLS] if y > 0 else zero
                right = xin[s, z, :, y * COLS + COLS : y * COLS + COLS + 128] if y < 3 else zero
                right = pltpu.roll(right, base, 1)
                left = pltpu.roll(left, (base + 4) % 128, 1)
                acc = jnp.where(jnp.logical_and(lane >= base, lane < base + 2), right, acc)
                acc = jnp.where(jnp.logical_and(lane >= base + 2, lane < base + 4), left, acc)
        yhs[y] = acc

    def hcopy(k, there):
        dst_sp = zsp if there else sp
        q = 4 * there + k
        return rcopy(
            yhs.at[after[k]], yh.at[sp, rows(ty)], hsend.at[q], hrecv.at[q], (dst_sp, tx, after[k])
        )

    for k in (1, 2, 3):
        go(hcopy(k, 0))
    for k in range(4):
        go(hcopy(k, 1))
    ownh = pltpu.make_async_copy(yhs.at[ty], yh.at[sp, rows(ty)], lsem.at[2])
    ownh.start()

    def pack_rows(first):
        for z in range(NZ):
            for s in range(2):
                xhs[4 * z + 2 * s : 4 * z + 2 * s + 2, :] = xin[s, z, first : first + 2, :]

    def xrows(first):
        return pl.ds(pl.multiple_of(first * 4, 8), 24)

    def xcopies(side, y):
        tx_to = tx + 1 if side == 0 else tx - 1
        half = 8 if side == 0 else 0
        q = 3 * (4 * side + y)
        tile = yhs.at[y, half : half + 8]
        return (
            rcopy(
                xhs.at[:, y * COLS : (y + 1) * COLS], xb.at[sp, side],
                xsend.at[q], xrecv.at[3 * side], (sp, tx_to, y),
            ),
            rcopy(tile, yhb.at[sp, side], xsend.at[q + 1], xrecv.at[3 * side + 1], (sp, tx_to, y)),
            rcopy(tile, yhb.at[sp, side], xsend.at[q + 2], xrecv.at[3 * side + 2], (zsp, tx_to, y)),
        )

    for side, cond, first in ((0, up, 14), (1, down, 0)):

        @pl.when(cond)
        def _(side=side, first=first):
            pack_rows(first)
            for y in range(4):
                for c in xcopies(side, y):
                    c.start()

    own.wait()
    ownh.wait()

    def xz():
        ref = xb.at[sp, :, xrows(p_there)]
        return rcopy(ref, ref, hsend.at[8], hrecv.at[8], zdev)

    def xc(q, who):
        ref = xb.at[who, :, xrows(p_here)]
        return rcopy(ref, ref, hsend.at[9 + q], hrecv.at[9 + q], cdev)

    def yc(q, who):
        ref = yh.at[who, 0:64]
        return rcopy(ref, ref, hsend.at[11 + q], hrecv.at[11 + q], cdev)

    def bc(q, who):
        return rcopy(yhb.at[who], yhb.at[who], hsend.at[13 + q], hrecv.at[13 + q], cdev)

    def pass_z(k, s):
        zcopy(k, s).wait_recv()
        if k:
            go(fcopy(k, s))
        else:
            go(cfcopy(k, s))

    for side, cond in ((0, tx > 0), (1, tx < 7)):

        @pl.when(cond)
        def _(side=side):
            for c in xcopies(side, 0):
                c.wait_recv()

    go(xz())
    go(xc(0, sp))
    go(bc(0, sp))
    go(bc(1, zsp))
    pass_z(2, 0)
    for k in (1, 3):
        ycopy(k).wait_recv()
        go(ccopy(k))
    pass_z(2, 1)
    for k in (1, 2, 3):
        hcopy(k, 0).wait_recv()
    for k in range(4):
        hcopy(k, 1).wait_recv()
    go(yc(0, sp))
    go(yc(1, zsp))
    pass_z(1, 0)
    ycopy(2).wait_recv()
    go(ccopy(2))
    pass_z(3, 0)
    pass_z(1, 1)
    pass_z(3, 1)
    xz().wait_recv()
    go(xc(1, zsp))
    for k, s in PIECES[:-2]:
        fcopy(k, s).wait_recv()
        go(cfcopy(k, s))
    pass_z(0, 0)
    pass_z(0, 1)

    for k in range(4):
        ccopy(k).wait_recv()
        for s in range(2):
            cfcopy(k, s).wait_recv()
    for q in range(2):
        xc(q, sp).wait_recv()
        yc(q, sp).wait_recv()
        bc(q, sp).wait_recv()
    for i in range(S):
        for z in range(NZ):
            r = 4 * z + 2 * (i % 2)
            m[i, 2 + z, 64:66, :] = xb[i // 2, 1, r : r + 2, :]
            m[i, 2 + z, 70:72, :] = xb[i // 2, 0, r : r + 2, :]
    row8 = lax.broadcasted_iota(jnp.int32, (8, 128), 0)
    lane8 = lax.broadcasted_iota(jnp.int32, (8, 128), 1)
    for q in range(4):
        yh[q, 64:72] = jnp.where(row8 < 4, yhb[q, 1], yhb[q, 0])

    def stage1(rt, _):
        tile = pl.ds(pl.multiple_of(rt * 8, 8), 8)
        dst = pl.ds(pl.multiple_of(rt * 8 + 8, 8), 8)
        for ct in range(2):
            v = [[m[i, 2 * sp + k, tile, ct * 128 : ct * 128 + 128] for k in range(6)] for i in range(S)]
            for f, (i, j) in enumerate(FIELDS):
                p = v[i] if j is None else [a * b for a, b in zip(v[i], v[j])]
                mid = (p[1] + p[2]) + (p[3] + p[4])
                zs[2 * f, ct, dst, :] = p[0] + mid
                zs[2 * f + 1, ct, dst, :] = mid + p[5]
        h = [
            pltpu.roll(yh[i // 2, tile, :], lax.rem(256 - 48 * (i % 2) - 8 * sp, 128), 1) for i in range(S)
        ]
        l4 = lax.rem(lane8, 4)
        for f, (i, j) in enumerate(FIELDS):
            p = h[i] if j is None else h[i] * h[j]
            p1 = p + pltpu.roll(p, 124, 1)
            p2 = p1 + pltpu.roll(p1, 120, 1)
            q = p2 + pltpu.roll(p, 112, 1)
            zh[f, dst, :] = (
                q
                + jnp.where(l4 == 1, pltpu.roll(q, 1, 1), 0.0)
                + jnp.where(l4 == 2, pltpu.roll(q, 127, 1), 0.0)
            )
        return 0

    lax.fori_loop(0, 9, stage1, 0)

    def wrap(f, _):
        zs[2 * f, :, 0:8, :] = zs[2 * f, :, 72:80, :]
        zs[2 * f + 1, :, 0:8, :] = zs[2 * f + 1, :, 72:80, :]
        zh[f, 0:8, :] = zh[f, 72:80, :]
        return 0

    lax.fori_loop(0, NF, wrap, 0)

    def span(pos, extent):
        return (jnp.minimum(pos + 2, extent - 1) - jnp.maximum(pos - 2, 0) + 1).astype(jnp.float32)

    def xsum(ref, x0):
        w = [ref[pl.ds(x0 * 8 + 6 + k, 8), :] for k in range(5)]
        return ((w[0] + w[1]) + (w[2] + w[3])) + w[4]

    def stage2(x0, _):
        out_rows = pl.ds(pl.multiple_of(x0 * 8, 8), 8)
        for g in range(2 * NF):
            for ct in range(2):
                xs[g * 8 : g * 8 + 8, ct * 128 : ct * 128 + 128] = xsum(zs.at[g, ct], x0)
        v = xs[...]
        hi = v.astype(jnp.bfloat16)
        rest = v - hi.astype(jnp.float32)
        mid = rest.astype(jnp.bfloat16)
        low = (rest - mid.astype(jnp.float32)).astype(jnp.bfloat16)
        hi, mid, low = (
            jnp.dot(t, band[...], preferred_element_type=jnp.float32) for t in (hi, mid, low)
        )
        ys[...] = hi + (mid + low)
        hx = [xsum(zh.at[f], x0) for f in range(NF)]
        cx_ = span(tx * ROWS + x0 * 8 + row8, NX)
        for p in range(2):
            cz = span(2 * sp + p, NZ)
            inv = [1.0 / (cx_ * span(ty * COLS + ct * 128 + lane8, NY) * cz) for ct in range(2)]

            def box(f):
                g = 8 * (2 * f + p)
                c = pltpu.roll(hx[f], 126 - 4 * p, 1)
                return (
                    (ys[g : g + 8, 0:128] + jnp.where(lane8 < 2, c, 0.0)) * inv[0],
                    (ys[g : g + 8, 128:256] + jnp.where(lane8 >= 126, c, 0.0)) * inv[1],
                )

            means = [box(i) for i in range(S)]
            var = []
            for i in range(S):
                sq = box(S + i)
                var.append(tuple(sq[t] - means[i][t] * means[i][t] + EPS for t in range(2)))
            for n, (i, j) in enumerate(PAIRS):
                pr = box(2 * S + n)
                for t in range(2):
                    cov = pr[t] - means[i][t] * means[j][t]
                    o_ref[n, p, out_rows, t * 128 : t * 128 + 128] = cov * lax.rsqrt(var[i][t] * var[j][t])
        return 0

    lax.fori_loop(0, 8, stage2, 0)
    for c in sent:
        c.wait_send()
    for side, cond in ((0, up), (1, down)):

        @pl.when(cond)
        def _(side=side):
            for y in range(4):
                for c in xcopies(side, y):
                    c.wait_send()


def shards(x):
    f32 = jnp.float32
    return pl.pallas_call(
        kernel,
        out_shape=jax.ShapeDtypeStruct((len(PAIRS), 2, ROWS, COLS), f32),
        in_specs=[pl.BlockSpec(memory_space=pltpu.VMEM)],
        out_specs=pl.BlockSpec(memory_space=pltpu.VMEM),
        scratch_shapes=[
            pltpu.VMEM((S, 12, 72, COLS), f32),
            pltpu.VMEM((3, 2, 6, BLK, COLS), f32),
            pltpu.VMEM((4, 72, 128), f32),
            pltpu.VMEM((4, 2, 8, 128), f32),
            pltpu.VMEM((4, 2, 32, COLS), f32),
            pltpu.VMEM((4, BLK, 128), f32),
            pltpu.VMEM((32, NY), f32),
            pltpu.VMEM((2 * NF, 2, 80, 128), f32),
            pltpu.VMEM((NF, 80, 128), f32),
            pltpu.VMEM((16 * NF, COLS), f32),
            pltpu.VMEM((16 * NF, COLS), f32),
            pltpu.VMEM((COLS, COLS), jnp.bfloat16),
        ]
        + [pltpu.SemaphoreType.DMA((n,)) for n in (8, 8, 4, 4, 8, 8, 12, 12, 15, 15, 24, 6, 3)],
        name="correlate",
        compiler_params=pltpu.CompilerParams(
            collective_id=0, has_side_effects=True, vmem_limit_bytes=48 << 20
        ),
    )(x)


def solution(mesh):
    return jax.shard_map(
        shards,
        mesh=mesh,
        in_specs=(P("sp", None, ("tx", "ty"), None),),
        out_specs=P(None, "sp", "tx", "ty"),
        check_vma=False,
    )
```

time: 125 us -> 48.2 us (0.39)
  Pallas kernels: 122 us -> 45 us
    pallas_call x1, Pallas kernels: 122 us -> 45 us  [shards(): pl.pallas_call(kernel, out_shape=jax.ShapeDtypeStruct((len(PAIRS), 2, ROW...]
where the time goes in v2:
time: 48.2 us; the launch traced here: 48.1 us
  Pallas kernels  45 us (93%)
  local copies, waits for them, and re-layouts  3.06 us (6%)
    pallas_call x1, Pallas kernels, shards(): pl.pallas_call(kernel, out_shape=jax.ShapeDtypeStruct((len(PAIRS), 2, ROW...  45 us
    unnamed x3, local copies, waits for them, and re-layouts  3.06 us

profile of v2, /device:TPU:1, one launch (start us, length us, event | category | flops | bytes accessed | tf_op | source)
XLA Modules:
  0.0 48.1 jit_solution(12078130329277870757)
XLA Ops:
  0.0 0.0 copy-start
  0.0 1.2 %copy-done = f32[2,8,16,1024]{3,2,1,0:T(8,128)S(1)} copy-done((f32[2,8,16,1024]{3,2,1,0:T(8,128)S(1)}, f32[2,8,16,1024]{3,2,1,0:T(8,128)}, u32[]{:S(2)}) %copy-start) | copy-done | bytes 1048600
  1.2 45.0 %correlate.1 = f32[28,2,64,256]{3,2,1,0:T(8,128)S(1)} custom-call(f32[2,8,16,1024]{3,2,1,0:T(8,128)S(1)} %copy-done), custom_call_target="tpu_custom_call" | custom-call | tf_op jit(solution)/shard_map/correlate/pallas_call | solution.py:378
  46.2 1.8 %copy.3 = f32[28,2,64,256]{3,2,1,0:T(8,128)} copy(f32[28,2,64,256]{3,2,1,0:T(8,128)S(1)} %correlate.1) | data formatting | bytes 7340032
Async XLA Ops:
  0.0 1.2 %copy-start = (f32[2,8,16,1024]{3,2,1,0:T(8,128)S(1)}, f32[2,8,16,1024]{3,2,1,0:T(8,128)}, u32[]{:S(2)}) copy-start(f32[2,8,16,1024]{3,2,1,0:T(8,128)} %xin.1) | copy-start | bytes 3145732

commit v3 on v2

v3 whole, which is shorter than its diff:
```python
import functools

import jax
import jax.numpy as jnp
from jax import lax
from jax.experimental import pallas as pl
from jax.experimental.pallas import tpu as pltpu
from jax.sharding import PartitionSpec as P

EPS = 1e-06
MESH = pl.DeviceIdType.MESH
S, NZ, NX, NY = 8, 8, 512, 1024
ROWS, COLS, BLK = 64, 256, 16
PAIRS = [(i, j) for i in range(S) for j in range(i + 1, S)]
FIELDS = [(i, None) for i in range(S)] + [(i, i) for i in range(S)] + PAIRS
NF = len(FIELDS)
Y_ORDER = ((1, 1), (3, 0), (1, 0), (3, 1), (2, 0), (2, 1))
UNITS = ((0, 0), (0, 1)) + Y_ORDER


def kernel(
    xin, o_ref, m, yh, xb, yhs, xhs, zs, zh, xs, ys, hs, hy, band, hband,
    ysend, yrecv, esend, erecv, zsend, zrecv, csend, crecv, hsend, hrecv, xsend, xrecv, lsem,
):
    sp, tx, ty = (lax.axis_index(a) for a in ("sp", "tx", "ty"))
    zhi = lax.div(sp, 2)
    core = lax.rem(sp, 2)
    zsp = lax.rem(sp + 2, 4)
    csp = sp + 1 - 2 * core
    p_here = 2 * zhi
    p_there = 2 - 2 * zhi
    p_extra = 6 * zhi

    def after(k):
        return lax.rem(ty + k, 4)

    def before(k):
        return lax.rem(ty + 4 - k, 4)

    up = jnp.logical_and(ty == 3, tx < 7)
    down = jnp.logical_and(ty == 0, tx > 0)

    barrier = pltpu.get_barrier_semaphore()

    def greet(*dev):
        pl.semaphore_signal(barrier, inc=1, device_id=dev, device_id_type=MESH)

    greet(zsp, tx, ty)
    greet(csp, tx, ty)
    for k in (2, 1, 3):
        greet(sp, tx, after(k))

    @pl.when(tx > 0)
    def _():
        greet(sp, tx - 1, 3)

    @pl.when(tx < 7)
    def _():
        greet(sp, tx + 1, 0)

    for s in range(S):
        m[s, 0:2] = jnp.zeros((2, 72, COLS), jnp.float32)
        m[s, 10:12] = jnp.zeros((2, 72, COLS), jnp.float32)

    @pl.when(tx == 0)
    def _():
        xb[sp, 0] = jnp.zeros((40, COLS), jnp.float32)

    @pl.when(tx == 7)
    def _():
        xb[sp, 1] = jnp.zeros((40, COLS), jnp.float32)

    r_at = lax.broadcasted_iota(jnp.int32, (COLS, COLS), 0)
    c_at = lax.broadcasted_iota(jnp.int32, (COLS, COLS), 1)
    band[...] = jnp.where(jnp.abs(r_at - c_at) <= 2, 1.0, 0.0).astype(jnp.bfloat16)

    r_at = lax.broadcasted_iota(jnp.int32, (128, COLS), 0)
    c_at = lax.broadcasted_iota(jnp.int32, (128, COLS), 1)
    plane, kind, first, col = lax.div(r_at, 4), lax.rem(r_at, 4), lax.div(c_at, 128), lax.rem(c_at, 128)
    ends = (
        ((kind == 0) & (col >= 126))
        | ((kind == 1) & (col == 127))
        | ((kind == 2) & (col == 0))
        | ((kind == 3) & (col <= 1))
    )
    hband[...] = jnp.where(
        ends & (plane >= first) & (plane <= first + 4), 1.0, 0.0
    ).astype(jnp.bfloat16)

    lane = lax.broadcasted_iota(jnp.int32, (BLK, 128), 1)
    for y in range(4):
        acc = jnp.zeros((BLK, 128), jnp.float32)
        for s in range(2):
            for z in range(NZ):
                base = 48 * s + 4 * (z + 2)
                zero = jnp.zeros((BLK, 128), jnp.float32)
                left = xin[s, z, :, y * COLS - 128 : y * COLS] if y > 0 else zero
                right = xin[s, z, :, y * COLS + COLS : y * COLS + COLS + 128] if y < 3 else zero
                right = pltpu.roll(right, base, 1)
                left = pltpu.roll(left, (base + 4) % 128, 1)
                acc = jnp.where(jnp.logical_and(lane >= base, lane < base + 2), right, acc)
                acc = jnp.where(jnp.logical_and(lane >= base + 2, lane < base + 4), left, acc)
        yhs[y] = acc

    def pack_rows(first, half):
        for y in range(4):
            for z in range(NZ):
                for s in range(2):
                    r = 4 * z + 2 * s + (8 if z >= 4 else 0)
                    xhs[y, r : r + 2, :] = xin[s, z, first : first + 2, y * COLS : (y + 1) * COLS]
            xhs[y, 16:24, 0:128] = yhs[y, half : half + 8]
            xhs[y, 16:24, 128:256] = jnp.zeros((8, 128), jnp.float32)

    @pl.when(up)
    def _():
        pack_rows(14, 8)

    @pl.when(down)
    def _():
        pack_rows(0, 0)

    pl.semaphore_wait(barrier, 5 + 4 * up.astype(jnp.int32) + 4 * down.astype(jnp.int32))

    def rcopy(src, dst, ss, rs, dev):
        return pltpu.make_async_remote_copy(
            src_ref=src, dst_ref=dst, send_sem=ss, recv_sem=rs, device_id=dev, device_id_type=MESH
        )

    def cols(y):
        return pl.ds(pl.multiple_of(y * COLS, COLS), COLS)

    def rows(b):
        return pl.ds(pl.multiple_of(b * BLK, BLK), BLK)

    def tile_of(b, t):
        return pl.ds(pl.multiple_of(b * BLK + 8 * t, 8), 8)

    zdev = (zsp, tx, ty)
    cdev = (csp, tx, ty)
    mine = pl.ds(2 * sp, 2)
    far = pl.ds(2 * zsp, 2)
    six = pl.ds(p_here + 2, 6)
    six_there = pl.ds(p_there + 2, 6)

    def ycopy(k, t):
        return rcopy(
            xin.at[:, pl.ds(p_there, 6), 8 * t : 8 * t + 8, cols(after(k))],
            m.at[mine, six_there, tile_of(ty, t)],
            ysend.at[2 * k + t], yrecv.at[2 * k + t], (sp, tx, after(k)),
        )

    def ecopy(k):
        return rcopy(
            xin.at[:, pl.ds(p_extra, 2), :, cols(after(k))],
            m.at[mine, pl.ds(p_extra + 2, 2), rows(ty)],
            esend.at[k], erecv.at[k], (sp, tx, after(k)),
        )

    def zcopy(k, t, first=False):
        dst = m.at[mine, six_there, tile_of(before(k), t)]
        src = xin.at[:, pl.ds(p_there, 6), 8 * t : 8 * t + 8, cols(ty)] if first else dst
        return rcopy(src, dst, zsend.at[2 * k + t], zrecv.at[2 * k + t], zdev)

    def ccopy(k, t, first=False):
        dst = m.at[mine, six, tile_of(before(k), t)]
        src = xin.at[:, pl.ds(p_here, 6), 8 * t : 8 * t + 8, cols(ty)] if first else dst
        return rcopy(src, dst, csend.at[2 * k + t], crecv.at[2 * k + t], cdev)

    def cfcopy(k, t):
        ref = m.at[far, six, tile_of(before(k), t)]
        return rcopy(ref, ref, csend.at[8 + 2 * k + t], crecv.at[8 + 2 * k + t], cdev)

    def hcopy(k):
        return rcopy(
            yhs.at[after(k)], yh.at[sp, rows(ty)], hsend.at[k], hrecv.at[k], (sp, tx, after(k))
        )

    def xcopy(side, y):
        return rcopy(
            xhs.at[y], xb.at[sp, side], xsend.at[4 * side + y], xrecv.at[side],
            (sp, tx + 1 if side == 0 else tx - 1, y),
        )

    zcopy(0, 0, True).start()
    zcopy(0, 1, True).start()
    for k, t in Y_ORDER[:2]:
        ycopy(k, t).start()
    for side, cond in ((0, up), (1, down)):

        @pl.when(cond)
        def _(side=side):
            for y in range(4):
                xcopy(side, y).start()

    for k in (2, 1, 3):
        hcopy(k).start()
    for k, t in Y_ORDER[2:4]:
        ycopy(k, t).start()
    ecopy(1).start()
    ecopy(3).start()
    for k, t in Y_ORDER[4:]:
        ycopy(k, t).start()
    ecopy(2).start()
    for t in range(2):
        ccopy(0, t, True).start()
    own = pltpu.make_async_copy(
        xin.at[:, pl.ds(p_here, 6), :, cols(ty)], m.at[mine, six, rows(ty)], lsem.at[0]
    )
    own.start()
    ownh = pltpu.make_async_copy(yhs.at[ty], yh.at[sp, rows(ty)], lsem.at[1])
    ownh.start()
    own.wait()
    ownh.wait()

    def xrows(first):
        return pl.ds(pl.multiple_of(first * 4, 8), 32)

    def xz():
        ref = xb.at[sp, :, xrows(p_there)]
        return rcopy(ref, ref, hsend.at[4], hrecv.at[4], zdev)

    def yz():
        ref = yh.at[sp, 0:64]
        return rcopy(ref, ref, hsend.at[5], hrecv.at[5], zdev)

    def xc(q, who):
        ref = xb.at[who, :, xrows(p_here)]
        return rcopy(ref, ref, hsend.at[6 + q], hrecv.at[6 + q], cdev)

    def yc(q, who):
        ref = yh.at[who, 0:64]
        return rcopy(ref, ref, hsend.at[8 + q], hrecv.at[8 + q], cdev)

    for k, t in Y_ORDER[:2]:
        ycopy(k, t).wait_recv()
        zcopy(k, t).start()
    for k in (1, 3, 2):
        hcopy(k).wait_recv()
    yz().start()
    yc(0, sp).start()
    for side, cond in ((0, tx > 0), (1, tx < 7)):

        @pl.when(cond)
        def _(side=side):
            xcopy(side, 0).wait_recv()

    xz().start()
    xc(0, sp).start()
    for k, t in Y_ORDER[2:4]:
        ycopy(k, t).wait_recv()
        zcopy(k, t).start()
    for t in range(2):
        zcopy(0, t).wait_recv()
        cfcopy(0, t).start()
    yz().wait_recv()
    yc(1, zsp).start()
    for k in (1, 3):
        ecopy(k).wait_recv()
        for t in range(2):
            ccopy(k, t).start()
    for q in range(2):
        yc(q, sp).wait_recv()
    for t in range(2):
        ccopy(0, t).wait_recv()
        cfcopy(0, t).wait_recv()

    row8 = lax.broadcasted_iota(jnp.int32, (8, 128), 0)
    lane8 = lax.broadcasted_iota(jnp.int32, (8, 128), 1)

    def stage1(rt, wrap=False):
        tile = pl.ds(pl.multiple_of(rt * 8, 8), 8)
        dsts = [pl.ds(pl.multiple_of(rt * 8 + 8, 8), 8)] + [pl.ds(0, 8)] * wrap
        for ct in range(2):
            v = [[m[i, 2 * sp + k, tile, ct * 128 : ct * 128 + 128] for k in range(6)] for i in range(S)]
            for f, (i, j) in enumerate(FIELDS):
                p = v[i] if j is None else [a * b for a, b in zip(v[i], v[j])]
                mid = (p[1] + p[2]) + (p[3] + p[4])
                for dst in dsts:
                    zs[2 * f, ct, dst, :] = p[0] + mid
                    zs[2 * f + 1, ct, dst, :] = mid + p[5]
        h = [
            pltpu.roll(yh[i // 2, tile, :], lax.rem(256 - 48 * (i % 2) - 8 * sp, 128), 1) for i in range(S)
        ]
        for f, (i, j) in enumerate(FIELDS):
            for dst in dsts:
                zh[f, dst, :] = h[i] if j is None else h[i] * h[j]

    def halos():
        xz().wait_recv()
        xc(1, zsp).start()
        for q in range(2):
            xc(q, sp).wait_recv()
        for i in range(S):
            for z in range(NZ):
                r = 4 * z + 2 * (i % 2) + (8 if z >= 4 else 0)
                m[i, 2 + z, 64:66, :] = xb[i // 2, 1, r : r + 2, :]
                m[i, 2 + z, 70:72, :] = xb[i // 2, 0, r : r + 2, :]
        for q in range(4):
            yh[q, 64:72] = jnp.where(row8 < 4, xb[q, 1, 16:24, 0:128], xb[q, 0, 16:24, 0:128])
        stage1(8, True)

    def span(pos, extent):
        return (jnp.minimum(pos + 2, extent - 1) - jnp.maximum(pos - 2, 0) + 1).astype(jnp.float32)

    def xsum(ref, x0):
        w = [ref[pl.ds(x0 * 8 + 6 + k, 8), :] for k in range(5)]
        return ((w[0] + w[1]) + (w[2] + w[3])) + w[4]

    def banded(v, w):
        hi = v.astype(jnp.bfloat16)
        rest = v - hi.astype(jnp.float32)
        mid = rest.astype(jnp.bfloat16)
        low = (rest - mid.astype(jnp.float32)).astype(jnp.bfloat16)
        hi, mid, low = (jnp.dot(q, w, preferred_element_type=jnp.float32) for q in (hi, mid, low))
        return hi + (mid + low)

    def stage2(x0):
        out_rows = pl.ds(pl.multiple_of(x0 * 8, 8), 8)
        for g in range(2 * NF):
            for ct in range(2):
                xs[g * 8 : g * 8 + 8, ct * 128 : ct * 128 + 128] = xsum(zs.at[g, ct], x0)
        for f in range(NF):
            hs[f * 8 : f * 8 + 8, :] = xsum(zh.at[f], x0)
        ys[...] = banded(xs[...], band[...])
        hy[...] = banded(hs[...], hband[...])
        cx_ = span(tx * ROWS + x0 * 8 + row8, NX)
        for p in range(2):
            cz = span(2 * sp + p, NZ)
            inv = [1.0 / (cx_ * span(ty * COLS + ct * 128 + lane8, NY) * cz) for ct in range(2)]

            def box(f):
                g = 8 * (2 * f + p)
                c = hy[8 * f : 8 * f + 8, 128 * p : 128 * p + 128]
                return (
                    (ys[g : g + 8, 0:128] + jnp.where(lane8 < 2, c, 0.0)) * inv[0],
                    (ys[g : g + 8, 128:256] + jnp.where(lane8 >= 126, c, 0.0)) * inv[1],
                )

            means = [box(i) for i in range(S)]
            var = []
            for i in range(S):
                sq = box(S + i)
                var.append(tuple(sq[t] - means[i][t] * means[i][t] + EPS for t in range(2)))
            for n, (i, j) in enumerate(PAIRS):
                pr = box(2 * S + n)
                for t in range(2):
                    cov = pr[t] - means[i][t] * means[j][t]
                    o_ref[n, p, out_rows, t * 128 : t * 128 + 128] = cov * lax.rsqrt(var[i][t] * var[j][t])

    def pick(u, values):
        return sum(v * (u == n).astype(jnp.int32) for n, v in enumerate(values) if v)

    def unit_of(r):
        k = lax.rem(ty + 4 - lax.div(r, 2), 4)
        q = 2 * k + lax.rem(r, 2)
        return pick(q, [UNITS.index((n // 2, n % 2)) for n in range(8)])

    def step(u, _):
        k, t = pick(u, [k for k, _ in UNITS]), pick(u, [t for _, t in UNITS])

        @pl.when(jnp.logical_and(u >= 2, u < 8))
        def _():
            zcopy(k, t).wait_recv()
            cfcopy(k, t).start()

        for n, (ky, t_y) in ((3, Y_ORDER[4]), (4, Y_ORDER[5])):

            @pl.when(u == n)
            def _(ky=ky, t_y=t_y):
                ycopy(ky, t_y).wait_recv()
                zcopy(ky, t_y).start()

        @pl.when(u == 5)
        def _():
            ecopy(2).wait_recv()
            for t in range(2):
                ccopy(2, t).start()

        @pl.when(u >= 1)
        def _():
            now = u - 1
            k, t = pick(now, [k for k, _ in UNITS]), pick(now, [t for _, t in UNITS])
            rt = 2 * before(k) + t

            @pl.when(now >= 2)
            def _():
                ccopy(k, t).wait_recv()
                cfcopy(k, t).wait_recv()

            stage1(rt)

            @pl.when(now == 1)
            def _():
                halos()

            def near(d, _):
                x0 = rt - 1 + d
                inside = jnp.logical_and(x0 >= 0, x0 < 8)
                done = jnp.maximum(unit_of(x0), jnp.maximum(unit_of(jnp.maximum(x0 - 1, 0)), unit_of(jnp.minimum(x0 + 1, 7))))

                @pl.when(jnp.logical_and(inside, done == now))
                def _():
                    stage2(x0)

                return 0

            lax.fori_loop(0, 3, near, 0)

        return 0

    lax.fori_loop(0, 9, step, 0)
    for k in range(4):
        for t in range(2):
            zcopy(k, t).wait_send()
            ccopy(k, t).wait_send()
            cfcopy(k, t).wait_send()
            if k:
                ycopy(k, t).wait_send()
        if k:
            ecopy(k).wait_send()
            hcopy(k).wait_send()
    xz().wait_send()
    yz().wait_send()
    for q in range(2):
        for c in (xc(q, sp), yc(q, sp)):
            c.wait_send()
    for side, cond in ((0, up), (1, down)):

        @pl.when(cond)
        def _(side=side):
            for y in range(4):
                xcopy(side, y).wait_send()


def shards(x):
    f32 = jnp.float32
    return pl.pallas_call(
        kernel,
        out_shape=jax.ShapeDtypeStruct((len(PAIRS), 2, ROWS, COLS), f32),
        in_specs=[pl.BlockSpec(memory_space=pltpu.VMEM)],
        out_specs=pl.BlockSpec(memory_space=pltpu.VMEM),
        scratch_shapes=[
            pltpu.VMEM((S, 12, 72, COLS), f32),
            pltpu.VMEM((4, 72, 128), f32),
            pltpu.VMEM((4, 2, 40, COLS), f32),
            pltpu.VMEM((4, BLK, 128), f32),
            pltpu.VMEM((4, 40, COLS), f32),
            pltpu.VMEM((2 * NF, 2, 80, 128), f32),
            pltpu.VMEM((NF, 80, 128), f32),
            pltpu.VMEM((16 * NF, COLS), f32),
            pltpu.VMEM((16 * NF, COLS), f32),
            pltpu.VMEM((8 * NF, 128), f32),
            pltpu.VMEM((8 * NF, COLS), f32),
            pltpu.VMEM((COLS, COLS), jnp.bfloat16),
            pltpu.VMEM((128, COLS), jnp.bfloat16),
        ]
        + [pltpu.SemaphoreType.DMA((n,)) for n in (8, 8, 4, 4, 8, 8, 16, 16, 10, 10, 8, 2, 2)],
        name="correlate",
        compiler_params=pltpu.CompilerParams(
            collective_id=0, has_side_effects=True, vmem_limit_bytes=48 << 20
        ),
    )(x)


def solution(mesh):
    return jax.shard_map(
        shards,
        mesh=mesh,
        in_specs=(P("sp", None, ("tx", "ty"), None),),
        out_specs=P(None, "sp", "tx", "ty"),
        check_vma=False,
    )
```

time: 48.2 us -> 39.4 us (0.82)
  Pallas kernels: 45 us -> 36.2 us
    pallas_call x1, Pallas kernels: 45 us -> 36.2 us  [shards(): pl.pallas_call(kernel, out_shape=jax.ShapeDtypeStruct((len(PAIRS), 2, ROW...]
where the time goes in v3:
time: 39.4 us; the launch traced here: 39.3 us
  Pallas kernels  36.2 us (92%)
  local copies, waits for them, and re-layouts  3.06 us (8%)
    pallas_call x1, Pallas kernels, shards(): pl.pallas_call(kernel, out_shape=jax.ShapeDtypeStruct((len(PAIRS), 2, ROW...  36.2 us
    unnamed x3, local copies, waits for them, and re-layouts  3.06 us

profile of v3, /device:TPU:1, one launch (start us, length us, event | category | flops | bytes accessed | tf_op | source)
XLA Modules:
  0.0 39.3 jit_solution(3841849103932761247)
XLA Ops:
  0.0 0.0 copy-start
  0.0 1.2 %copy-done = f32[2,8,16,1024]{3,2,1,0:T(8,128)S(1)} copy-done((f32[2,8,16,1024]{3,2,1,0:T(8,128)S(1)}, f32[2,8,16,1024]{3,2,1,0:T(8,128)}, u32[]{:S(2)}) %copy-start) | copy-done | bytes 1048600
  1.2 36.2 %correlate.1 = f32[28,2,64,256]{3,2,1,0:T(8,128)S(1)} custom-call(f32[2,8,16,1024]{3,2,1,0:T(8,128)S(1)} %copy-done), custom_call_target="tpu_custom_call" | custom-call | tf_op jit(solution)/shard_map/correlate/pallas_call | solution.py:437
  37.5 1.8 %copy.3 = f32[28,2,64,256]{3,2,1,0:T(8,128)} copy(f32[28,2,64,256]{3,2,1,0:T(8,128)S(1)} %correlate.1) | data formatting | bytes 7340032
Async XLA Ops:
  0.0 1.2 %copy-start = (f32[2,8,16,1024]{3,2,1,0:T(8,128)S(1)}, f32[2,8,16,1024]{3,2,1,0:T(8,128)}, u32[]{:S(2)}) copy-start(f32[2,8,16,1024]{3,2,1,0:T(8,128)} %xin.1) | copy-start | bytes 3145732

commit v4 on v3

v4 whole, which is shorter than its diff:
```python
import jax
import jax.numpy as jnp
from jax import lax
from jax.experimental import pallas as pl
from jax.experimental.pallas import tpu as pltpu
from jax.sharding import PartitionSpec as P

EPS = 1e-06
MESH = pl.DeviceIdType.MESH
S, NZ, NX, NY = 8, 8, 512, 1024
ROWS, COLS, BLK = 64, 256, 16
PAIRS = [(i, j) for i in range(S) for j in range(i + 1, S)]
FIELDS = [(i, None) for i in range(S)] + [(i, i) for i in range(S)] + PAIRS
NF = len(FIELDS)
Y_ORDER = ((1, 1), (3, 0), (1, 0), (3, 1))
K_UNITS = (0, 0, 1, 3, 1, 3, 2, 2)
T_UNITS = (0, 1, 1, 0, 0, 1)
GROUPS = (((5, 0), (6, 5), (7, 3)), ((4, 0), (5, 2), (7, 5)), ((4, 3), (5, 5), (7, 0)), ((4, 5), (6, 0), (7, 2)))
GROUP = 3
HALO_UNIT = 3


def kernel(
    x, o_ref, xin, m, yh, xb, yhs, xhs, yz, lhs, rhs, tmp,
    ysend, yrecv, esend, erecv, zsend, zrecv, csend, crecv, hsend, hrecv, xsend, xrecv, lsem,
):
    sp, tx, ty = (lax.axis_index(a) for a in ("sp", "tx", "ty"))
    zhi = lax.div(sp, 2)
    core = lax.rem(sp, 2)
    zsp = lax.rem(sp + 2, 4)
    csp = sp + 1 - 2 * core
    p_here = 2 * zhi
    p_there = 2 - 2 * zhi
    p_extra = 6 * zhi

    def after(k):
        return lax.rem(ty + k, 4)

    def before(k):
        return lax.rem(ty + 4 - k, 4)

    up = jnp.logical_and(ty == 3, tx < 7)
    down = jnp.logical_and(ty == 0, tx > 0)

    barrier = pltpu.get_barrier_semaphore()

    def greet(*dev):
        pl.semaphore_signal(barrier, inc=1, device_id=dev, device_id_type=MESH)

    for k in (2, 1, 3):
        greet(sp, tx, after(k))
    greet(zsp, tx, ty)
    greet(csp, tx, ty)

    @pl.when(tx > 0)
    def _():
        greet(sp, tx - 1, 3)

    @pl.when(tx < 7)
    def _():
        greet(sp, tx + 1, 0)

    load = pltpu.make_async_copy(x, xin, lsem.at[0])
    load.start()
    pl.semaphore_wait(barrier, 5 + 4 * up.astype(jnp.int32) + 4 * down.astype(jnp.int32))

    def rcopy(src, dst, ss, rs, dev):
        return pltpu.make_async_remote_copy(
            src_ref=src, dst_ref=dst, send_sem=ss, recv_sem=rs, device_id=dev, device_id_type=MESH
        )

    def cols(y):
        return pl.ds(pl.multiple_of(y * COLS, COLS), COLS)

    def tile_of(b, t):
        return pl.ds(pl.multiple_of(b * BLK + 8 * t, 8), 8)

    def pick(u, values):
        return sum(v * (u == n).astype(jnp.int32) for n, v in enumerate(values))

    t_sent, t_got = pick(ty, (0, 0, 1)), pick(ty, (1,))

    def eight(b):
        return pl.ds(pl.multiple_of(b * 8, 8), 8)

    zdev = (zsp, tx, ty)
    cdev = (csp, tx, ty)
    mine = pl.ds(2 * sp, 2)
    far = pl.ds(2 * zsp, 2)
    six = pl.ds(p_here + 2, 6)
    six_there = pl.ds(p_there + 2, 6)
    own_rows = pl.ds(pl.multiple_of(ty * BLK, BLK), BLK)

    def ycopy(k, t):
        return rcopy(
            x.at[:, pl.ds(p_there, 6), eight(t), cols(after(k))],
            m.at[mine, six_there, tile_of(ty, t)],
            ysend.at[2 * k + t], yrecv.at[2 * k + t], (sp, tx, after(k)),
        )

    def ecopy(k):
        return rcopy(
            x.at[:, pl.ds(p_extra, 2), :, cols(after(k))],
            m.at[mine, pl.ds(p_extra + 2, 2), own_rows],
            esend.at[k], erecv.at[k], (sp, tx, after(k)),
        )

    def zcopy(k, t, first=False):
        dst = m.at[mine, six_there, tile_of(before(k), t)]
        src = x.at[:, pl.ds(p_there, 6), 8 * t : 8 * t + 8, cols(ty)] if first else dst
        return rcopy(src, dst, zsend.at[2 * k + t], zrecv.at[2 * k + t], zdev)

    def ccopy(k, t, first=False):
        dst = m.at[mine, six, tile_of(before(k), t)]
        src = x.at[:, pl.ds(p_here, 6), 8 * t : 8 * t + 8, cols(ty)] if first else dst
        return rcopy(src, dst, csend.at[2 * k + t], crecv.at[2 * k + t], cdev)

    def cfcopy(k, t):
        ref = m.at[far, six, tile_of(before(k), t)]
        return rcopy(ref, ref, csend.at[8 + 2 * k + t], crecv.at[8 + 2 * k + t], cdev)

    def hcopy(k):
        return rcopy(yhs.at[after(k)], yh.at[sp, eight(ty)], hsend.at[k], hrecv.at[k], (sp, tx, after(k)))

    def xcopies(side, y):
        dev = (sp, tx + 1 if side == 0 else tx - 1, y)
        q = 2 * (4 * side + y)
        return (
            rcopy(xhs.at[y], xb.at[sp, side], xsend.at[q], xrecv.at[2 * side], dev),
            rcopy(
                yhs.at[y], yh.at[sp, 32 + 8 * side : 40 + 8 * side],
                xsend.at[q + 1], xrecv.at[2 * side + 1], dev,
            ),
        )

    def xrows(first):
        return pl.ds(pl.multiple_of(first * 4, 8), 24)

    def xz():
        ref = xb.at[sp, :, xrows(p_there)]
        return rcopy(ref, ref, hsend.at[4], hrecv.at[4], zdev)

    def yzcopy():
        return rcopy(yh.at[sp], yh.at[sp], hsend.at[5], hrecv.at[5], zdev)

    def xc(q, who):
        ref = xb.at[who, :, xrows(p_here)]
        return rcopy(ref, ref, hsend.at[6 + q], hrecv.at[6 + q], cdev)

    def yc(q, who):
        return rcopy(yh.at[who], yh.at[who], hsend.at[8 + q], hrecv.at[8 + q], cdev)

    zcopy(0, 0, True).start()
    zcopy(0, 1, True).start()
    for k, t in Y_ORDER[:2]:
        ycopy(k, t).start()

    load.wait()
    row8 = lax.broadcasted_iota(jnp.int32, (8, 128), 0)
    lane8 = lax.broadcasted_iota(jnp.int32, (8, 128), 1)
    zero = jnp.zeros((8, 128), jnp.float32)
    for y in range(4):
        acc = zero
        for t in range(2):
            for s in range(2):
                for z in range(NZ):
                    base = 64 * t + 32 * s + 4 * z
                    at = slice(8 * t, 8 * t + 8)
                    left = xin[s, z, at, y * COLS - 128 : y * COLS] if y > 0 else zero
                    right = xin[s, z, at, y * COLS + COLS : y * COLS + COLS + 128] if y < 3 else zero
                    if y < 3:
                        right = pltpu.roll(right, base, 1) if base else right
                    if y > 0:
                        left = pltpu.roll(left, (base + 4) % 128, 1) if base != 124 else left
                    acc = jnp.where(jnp.logical_and(lane8 >= base, lane8 < base + 2), right, acc)
                    acc = jnp.where(jnp.logical_and(lane8 >= base + 2, lane8 < base + 4), left, acc)
        yhs[y] = acc

    def pack_rows(first):
        for y in range(4):
            for z in range(NZ):
                for s in range(2):
                    r = 4 * z + 2 * s
                    xhs[y, r : r + 2, :] = xin[s, z, first : first + 2, y * COLS : (y + 1) * COLS]

    for side, cond, first in ((0, up, 14), (1, down, 0)):

        @pl.when(cond)
        def _(side=side, first=first):
            pack_rows(first)
            for y in range(4):
                for c in xcopies(side, y):
                    c.start()

    for k in (2, 1, 3):
        hcopy(k).start()
    for k, t in Y_ORDER[2:]:
        ycopy(k, t).start()
    ecopy(1).start()
    ecopy(3).start()
    ycopy(2, t_sent).start()
    ycopy(2, 1 - t_sent).start()
    ecopy(2).start()
    for t in range(2):
        ccopy(0, t, True).start()
    own = pltpu.make_async_copy(
        x.at[:, pl.ds(p_here, 6), :, cols(ty)], m.at[mine, six, own_rows], lsem.at[1]
    )
    own.start()
    yh[sp, eight(ty)] = yhs[ty]

    for s in range(S):
        m[s, 0:2] = jnp.zeros((2, 72, COLS), jnp.float32)
        m[s, 10:12] = jnp.zeros((2, 72, COLS), jnp.float32)

    for side, cond in ((0, tx == 0), (1, tx == 7)):

        @pl.when(cond)
        def _(side=side):
            xb[sp, side] = jnp.zeros((32, COLS), jnp.float32)
            yh[sp, 32 + 8 * side : 40 + 8 * side] = zero

    for k, t in Y_ORDER[:2]:
        ycopy(k, t).wait_recv()
        zcopy(k, t).start()
    for k in (1, 3, 2):
        hcopy(k).wait_recv()
    for side, cond in ((0, tx > 0), (1, tx < 7)):

        @pl.when(cond)
        def _(side=side):
            for c in xcopies(side, 0):
                c.wait_recv()

    yzcopy().start()
    yc(0, sp).start()
    xz().start()
    xc(0, sp).start()
    for k, t in Y_ORDER[2:4]:
        ycopy(k, t).wait_recv()
        zcopy(k, t).start()

    r_at = lax.broadcasted_iota(jnp.int32, (COLS, COLS), 0)
    c_at = lax.broadcasted_iota(jnp.int32, (COLS, COLS), 1)
    band = jnp.where(jnp.abs(r_at - c_at) <= 2, 1.0, 0.0).astype(jnp.bfloat16)
    r_at = lax.broadcasted_iota(jnp.int32, (128, COLS), 0)
    c_at = lax.broadcasted_iota(jnp.int32, (128, COLS), 1)
    plane, kind = lax.div(r_at, 4), lax.rem(r_at, 4)
    ends = (
        ((kind == 0) & (c_at >= COLS - 2))
        | ((kind == 1) & (c_at == COLS - 1))
        | ((kind == 2) & (c_at == 0))
        | ((kind == 3) & (c_at <= 1))
    )
    for p in range(2):
        part = jnp.where(ends & (plane >= p) & (plane <= p + 4), 1.0, 0.0).astype(jnp.bfloat16)
        for q in range(3):
            rhs[p, 256 * q : 256 * q + 256, :] = band
            rhs[p, 768 + 128 * q : 896 + 128 * q, :] = part

    for t in range(2):
        zcopy(0, t).wait_recv()
        cfcopy(0, t).start()
    yzcopy().wait_recv()
    yc(1, zsp).start()
    for k in (1, 3):
        ecopy(k).wait_recv()
        for t in range(2):
            ccopy(k, t).start()
    own.wait()
    for q in range(2):
        yc(q, sp).wait_recv()
    for t in range(2):
        ccopy(0, t).wait_recv()
        cfcopy(0, t).wait_recv()

    def split(v):
        hi = v.astype(jnp.bfloat16)
        rest = v - hi.astype(jnp.float32)
        mid = rest.astype(jnp.bfloat16)
        return hi, mid, (rest - mid.astype(jnp.float32)).astype(jnp.bfloat16)

    def halo_cols(i, rows, t):
        h = pltpu.roll(yh[i // 2, rows, :], lax.rem(264 - 64 * t - 32 * (i % 2) - 8 * sp, 128), 1)
        at = 2 * sp - 2 + lax.div(lane8, 4)
        return jnp.where((at >= 0) & (at < NZ), h, 0.0)

    def stage1(rt, h, wrap=False):
        tile = pl.ds(pl.multiple_of(rt * 8, 8), 8)
        dsts = [pl.ds(pl.multiple_of(rt * 8 + 8, 8), 8)] + [pl.ds(0, 8)] * wrap
        for ct in range(2):
            v = [[m[i, 2 * sp + k, tile, ct * 128 : ct * 128 + 128] for k in range(6)] for i in range(S)]
            for f in range(0, NF, 2):
                sums = [[], []]
                for i, j in FIELDS[f : f + 2]:
                    p = v[i] if j is None else [a * b for a, b in zip(v[i], v[j])]
                    mid = (p[1] + p[2]) + (p[3] + p[4])
                    sums[0].append(p[0] + mid)
                    sums[1].append(mid + p[5])
                for p in range(2):
                    for q, part in enumerate(split(jnp.concatenate(sums[p], 0))):
                        at = 256 * q + 128 * ct
                        lhs[p, 8 * f : 8 * f + 16, at : at + 128] = part
        for f in range(0, NF, 2):
            hv = [h[i] if j is None else h[i] * h[j] for i, j in FIELDS[f : f + 2]]
            for q, part in enumerate(split(jnp.concatenate(hv, 0))):
                for p in range(2):
                    lhs[p, 8 * f : 8 * f + 16, 768 + 128 * q : 896 + 128 * q] = part
        for p in range(2):
            r = jnp.dot(lhs[p], rhs[p], preferred_element_type=jnp.float32)
            for f in range(NF):
                for ct in range(2):
                    for dst in dsts:
                        yz[2 * f + p, ct, dst, :] = r[8 * f : 8 * f + 8, 128 * ct : 128 * ct + 128]

    def halos():
        xz().wait_recv()
        xc(1, zsp).start()
        for q in range(2):
            xc(q, sp).wait_recv()
        for i in range(S):
            for z in range(NZ):
                r = 4 * z + 2 * (i % 2)
                m[i, 2 + z, 64:66, :] = xb[i // 2, 1, r : r + 2, :]
                m[i, 2 + z, 70:72, :] = xb[i // 2, 0, r : r + 2, :]
        h = [
            jnp.where(row8 < 4, halo_cols(i, slice(40, 48), 0), halo_cols(i, slice(32, 40), 1)) for i in range(S)
        ]
        stage1(8, h, True)

    def span(pos, extent):
        return (jnp.minimum(pos + 2, extent - 1) - jnp.maximum(pos - 2, 0) + 1).astype(jnp.float32)

    def stage2(x0):
        start = x0 * 8
        for p in range(2):
            cz = span(2 * sp + p, NZ)
            for ct in range(2):
                cy = span(ty * COLS + ct * 128 + lane8, NY) * cz
                inv = [1.0 / (span(tx * ROWS + start + row8 * GROUP + q, NX) * cy) for q in range(GROUP)]

                def box(f):
                    w = [yz[2 * f + p, ct, pl.ds(start + 6 + q, 8, stride=GROUP), :] for q in range(GROUP + 4)]
                    a = [w[q] + w[q + 1] for q in range(GROUP + 3)]
                    return [((a[q] + a[q + 2]) + w[q + 4]) * inv[q] for q in range(GROUP)]

                means = [box(i) for i in range(S)]
                var = [[b - u * u + EPS for b, u in zip(box(S + i), means[i])] for i in range(S)]
                for n, (i, j) in enumerate(PAIRS):
                    b = box(2 * S + n)
                    for q in range(GROUP):
                        cov = b[q] - means[i][q] * means[j][q]
                        tmp[n, pl.ds(q, 8, stride=GROUP), :] = cov * lax.rsqrt(var[i][q] * var[j][q])
                for n in range(len(PAIRS)):
                    o_ref[n, p, pl.ds(pl.multiple_of(start, 8), 8 * GROUP), ct * 128 : ct * 128 + 128] = tmp[n]

    def unit(u):
        return pick(u, K_UNITS), pick(u, T_UNITS + (t_got, 1 - t_got))

    def step(u, _):
        @pl.when(jnp.logical_and(u >= 2, u < 8))
        def _():
            k, t = unit(u)
            zcopy(k, t).wait_recv()
            cfcopy(k, t).start()

        for n, t in ((3, t_got), (4, 1 - t_got)):

            @pl.when(u == n)
            def _(t=t):
                ycopy(2, t).wait_recv()
                zcopy(2, t).start()

        @pl.when(u == 5)
        def _():
            ecopy(2).wait_recv()
            for t in range(2):
                ccopy(2, t).start()

        @pl.when(u >= 1)
        def _():
            k, t = unit(u - 1)
            b = before(k)

            @pl.when(u >= 3)
            def _():
                ccopy(k, t).wait_recv()
                cfcopy(k, t).wait_recv()

            stage1(2 * b + t, [halo_cols(i, eight(b), t) for i in range(S)])

            @pl.when(u - 1 == HALO_UNIT)
            def _():
                halos()

            group = sum(
                (g0 + 1) * ((ty == y) & (u - 1 == n)).astype(jnp.int32) for y in range(4) for n, g0 in GROUPS[y]
            )

            @pl.when(group > 0)
            def _():
                stage2(group - 1)

        return 0

    lax.fori_loop(0, 9, step, 0)

    for k in range(4):
        for t in range(2):
            zcopy(k, t).wait_send()
            ccopy(k, t).wait_send()
            cfcopy(k, t).wait_send()
            if k:
                ycopy(k, t).wait_send()
        if k:
            ecopy(k).wait_send()
            hcopy(k).wait_send()
    xz().wait_send()
    yzcopy().wait_send()
    for q in range(2):
        for c in (xc(q, sp), yc(q, sp)):
            c.wait_send()
    for side, cond in ((0, up), (1, down)):

        @pl.when(cond)
        def _(side=side):
            for y in range(4):
                for c in xcopies(side, y):
                    c.wait_send()


def shards(x):
    f32 = jnp.float32
    return pl.pallas_call(
        kernel,
        out_shape=jax.ShapeDtypeStruct((len(PAIRS), 2, ROWS, COLS), f32),
        in_specs=[pl.BlockSpec(memory_space=pltpu.HBM)],
        out_specs=pl.BlockSpec(memory_space=pltpu.VMEM),
        scratch_shapes=[
            pltpu.VMEM((2, NZ, BLK, NY), f32),
            pltpu.VMEM((S, 12, 72, COLS), f32),
            pltpu.VMEM((4, 48, 128), f32),
            pltpu.VMEM((4, 2, 32, COLS), f32),
            pltpu.VMEM((4, 8, 128), f32),
            pltpu.VMEM((4, 32, COLS), f32),
            pltpu.VMEM((2 * NF, 2, 80, 128), f32),
            pltpu.VMEM((2, 8 * NF, 1152), jnp.bfloat16),
            pltpu.VMEM((2, 1152, COLS), jnp.bfloat16),
            pltpu.VMEM((len(PAIRS), 8 * GROUP, 128), f32),
        ]
        + [pltpu.SemaphoreType.DMA((n,)) for n in (8, 8, 4, 4, 8, 8, 16, 16, 10, 10, 16, 4, 2)],
        name="correlate",
        compiler_params=pltpu.CompilerParams(
            collective_id=0, has_side_effects=True, vmem_limit_bytes=48 << 20
        ),
    )(pltpu.with_memory_space_constraint(x, pltpu.HBM))


def solution(mesh):
    return jax.shard_map(
        shards,
        mesh=mesh,
        in_specs=(P("sp", None, ("tx", "ty"), None),),
        out_specs=P(None, "sp", "tx", "ty"),
        check_vma=False,
    )
```

time: 39.4 us -> 37 us (0.939)
  local copies, waits for them, and re-layouts: 3.06 us -> 1.84 us
  Pallas kernels: 36.2 us -> 35 us
    unnamed x3 -> x1, local copies, waits for them, and re-layouts: 3.06 us -> 1.84 us
    pallas_call x1, Pallas kernels: 36.2 us -> 35 us  [shards(): pl.pallas_call(kernel, out_shape=jax.ShapeDtypeStruct((len(PAIRS), 2, ROW...]
where the time goes in v4:
time: 37 us; the launch traced here: 36.9 us
  Pallas kernels  35 us (95%)
  local copies, waits for them, and re-layouts  1.84 us (5%)
    pallas_call x1, Pallas kernels, shards(): pl.pallas_call(kernel, out_shape=jax.ShapeDtypeStruct((len(PAIRS), 2, ROW...  35 us
    unnamed x1, local copies, waits for them, and re-layouts  1.84 us

profile of v4, /device:TPU:1, one launch (start us, length us, event | category | flops | bytes accessed | tf_op | source)
XLA Modules:
  0.0 36.9 jit_solution(18317906020049156019)
XLA Ops:
  0.0 35.0 %correlate.1 = f32[28,2,64,256]{3,2,1,0:T(8,128)S(1)} custom-call(f32[2,8,16,1024]{3,2,1,0:T(8,128)} %x.1), custom_call_target="tpu_custom_call" | custom-call | tf_op jit(solution)/shard_map/correlate/pallas_call | solution.py:434
  35.0 1.8 %copy.3 = f32[28,2,64,256]{3,2,1,0:T(8,128)} copy(f32[28,2,64,256]{3,2,1,0:T(8,128)S(1)} %correlate.1) | data formatting | bytes 7340032

commit v5 on v4

--- a/solution.py
+++ b/solution.py
@@ -13,11 +13,10 @@
 FIELDS = [(i, None) for i in range(S)] + [(i, i) for i in range(S)] + PAIRS
 NF = len(FIELDS)
 Y_ORDER = ((1, 1), (3, 0), (1, 0), (3, 1))
-K_UNITS = (0, 0, 1, 3, 1, 3, 2, 2)
-T_UNITS = (0, 1, 1, 0, 0, 1)
 GROUPS = (((5, 0), (6, 5), (7, 3)), ((4, 0), (5, 2), (7, 5)), ((4, 3), (5, 5), (7, 0)), ((4, 5), (6, 0), (7, 2)))
 GROUP = 3
-HALO_UNIT = 3
+COLUMNS, CORNERS = slice(0, 32), slice(32, 48)
+HALO_UNIT = 4
 
 
 def kernel(
@@ -49,6 +48,7 @@
 
     for k in (2, 1, 3):
         greet(sp, tx, after(k))
+        greet(zsp, tx, after(k))
     greet(zsp, tx, ty)
     greet(csp, tx, ty)
 
@@ -62,7 +62,7 @@
 
     load = pltpu.make_async_copy(x, xin, lsem.at[0])
     load.start()
-    pl.semaphore_wait(barrier, 5 + 4 * up.astype(jnp.int32) + 4 * down.astype(jnp.int32))
+    pl.semaphore_wait(barrier, 8 + 4 * up.astype(jnp.int32) + 4 * down.astype(jnp.int32))
 
     def rcopy(src, dst, ss, rs, dev):
         return pltpu.make_async_remote_copy(
@@ -79,6 +79,9 @@
         return sum(v * (u == n).astype(jnp.int32) for n, v in enumerate(values))
 
     t_sent, t_got = pick(ty, (0, 0, 1)), pick(ty, (1,))
+    turn = pick(ty, (1,))
+    k_units = (0, 0) + (1 + 2 * turn, 3 - 2 * turn) * 2 + (2, 2)
+    t_units = (0, 1, 1 - turn, turn, turn, 1 - turn, t_got, 1 - t_got)
 
     def eight(b):
         return pl.ds(pl.multiple_of(b * 8, 8), 8)
@@ -119,8 +122,10 @@
         ref = m.at[far, six, tile_of(before(k), t)]
         return rcopy(ref, ref, csend.at[8 + 2 * k + t], crecv.at[8 + 2 * k + t], cdev)
 
-    def hcopy(k):
-        return rcopy(yhs.at[after(k)], yh.at[sp, eight(ty)], hsend.at[k], hrecv.at[k], (sp, tx, after(k)))
+    def hcopy(k, there):
+        dev = (zsp if there else sp, tx, after(k))
+        q = 4 * there + k
+        return rcopy(yhs.at[after(k)], yh.at[sp, eight(ty)], hsend.at[q], hrecv.at[q], dev)
 
     def xcopies(side, y):
         dev = (sp, tx + 1 if side == 0 else tx - 1, y)
@@ -138,20 +143,22 @@
 
     def xz():
         ref = xb.at[sp, :, xrows(p_there)]
-        return rcopy(ref, ref, hsend.at[4], hrecv.at[4], zdev)
+        return rcopy(ref, ref, hsend.at[8], hrecv.at[8], zdev)
 
     def yzcopy():
-        return rcopy(yh.at[sp], yh.at[sp], hsend.at[5], hrecv.at[5], zdev)
+        ref = yh.at[sp, CORNERS]
+        return rcopy(ref, ref, hsend.at[9], hrecv.at[9], zdev)
 
     def xc(q, who):
         ref = xb.at[who, :, xrows(p_here)]
-        return rcopy(ref, ref, hsend.at[6 + q], hrecv.at[6 + q], cdev)
-
-    def yc(q, who):
-        return rcopy(yh.at[who], yh.at[who], hsend.at[8 + q], hrecv.at[8 + q], cdev)
+        return rcopy(ref, ref, hsend.at[10 + q], hrecv.at[10 + q], cdev)
+
+    def yc(q, who, part):
+        ref = yh.at[who, part]
+        q = q + (12 if part is COLUMNS else 14)
+        return rcopy(ref, ref, hsend.at[q], hrecv.at[q], cdev)
 
     zcopy(0, 0, True).start()
-    zcopy(0, 1, True).start()
     for k, t in Y_ORDER[:2]:
         ycopy(k, t).start()
 
@@ -176,6 +183,12 @@
                     acc = jnp.where(jnp.logical_and(lane8 >= base + 2, lane8 < base + 4), left, acc)
         yhs[y] = acc
 
+    yh[sp, eight(ty)] = yhs[ty]
+    for k in (2, 1, 3):
+        hcopy(k, 1).start()
+        hcopy(k, 0).start()
+    hcopy(0, 1).start()
+
     def pack_rows(first):
         for y in range(4):
             for z in range(NZ):
@@ -192,8 +205,7 @@
                 for c in xcopies(side, y):
                     c.start()
 
-    for k in (2, 1, 3):
-        hcopy(k).start()
+    zcopy(0, 1, True).start()
     for k, t in Y_ORDER[2:]:
         ycopy(k, t).start()
     ecopy(1).start()
@@ -207,7 +219,6 @@
         x.at[:, pl.ds(p_here, 6), :, cols(ty)], m.at[mine, six, own_rows], lsem.at[1]
     )
     own.start()
-    yh[sp, eight(ty)] = yhs[ty]
 
     for s in range(S):
         m[s, 0:2] = jnp.zeros((2, 72, COLS), jnp.float32)
@@ -220,11 +231,17 @@
             xb[sp, side] = jnp.zeros((32, COLS), jnp.float32)
             yh[sp, 32 + 8 * side : 40 + 8 * side] = zero
 
-    for k, t in Y_ORDER[:2]:
+    for k, t in list(zip(k_units, t_units))[2:4]:
         ycopy(k, t).wait_recv()
         zcopy(k, t).start()
-    for k in (1, 3, 2):
-        hcopy(k).wait_recv()
+    for k in range(4):
+        hcopy(k, 1).wait_recv()
+        if k:
+            hcopy(k, 0).wait_recv()
+    yc(0, sp, COLUMNS).start()
+    yc(1, zsp, COLUMNS).start()
+    zcopy(0, 0).wait_recv()
+    cfcopy(0, 0).start()
     for side, cond in ((0, tx > 0), (1, tx < 7)):
 
         @pl.when(cond)
@@ -232,11 +249,11 @@
             for c in xcopies(side, 0):
                 c.wait_recv()
 
+    xz().start()
     yzcopy().start()
-    yc(0, sp).start()
-    xz().start()
     xc(0, sp).start()
-    for k, t in Y_ORDER[2:4]:
+    yc(0, sp, CORNERS).start()
+    for k, t in list(zip(k_units, t_units))[4:6]:
         ycopy(k, t).wait_recv()
         zcopy(k, t).start()
 
@@ -258,21 +275,11 @@
             rhs[p, 256 * q : 256 * q + 256, :] = band
             rhs[p, 768 + 128 * q : 896 + 128 * q, :] = part
 
-    for t in range(2):
-        zcopy(0, t).wait_recv()
-        cfcopy(0, t).start()
-    yzcopy().wait_recv()
-    yc(1, zsp).start()
-    for k in (1, 3):
-        ecopy(k).wait_recv()
-        for t in range(2):
-            ccopy(k, t).start()
+    zcopy(0, 1).wait_recv()
+    cfcopy(0, 1).start()
     own.wait()
     for q in range(2):
-        yc(q, sp).wait_recv()
-    for t in range(2):
-        ccopy(0, t).wait_recv()
-        cfcopy(0, t).wait_recv()
+        yc(q, sp, COLUMNS).wait_recv()
 
     def split(v):
         hi = v.astype(jnp.bfloat16)
@@ -314,10 +321,9 @@
                         yz[2 * f + p, ct, dst, :] = r[8 * f : 8 * f + 8, 128 * ct : 128 * ct + 128]
 
     def halos():
-        xz().wait_recv()
-        xc(1, zsp).start()
         for q in range(2):
             xc(q, sp).wait_recv()
+            yc(q, sp, CORNERS).wait_recv()
         for i in range(S):
             for z in range(NZ):
                 r = 4 * z + 2 * (i % 2)
@@ -355,7 +361,7 @@
                     o_ref[n, p, pl.ds(pl.multiple_of(start, 8), 8 * GROUP), ct * 128 : ct * 128 + 128] = tmp[n]
 
     def unit(u):
-        return pick(u, K_UNITS), pick(u, T_UNITS + (t_got, 1 - t_got))
+        return pick(u, k_units), pick(u, t_units)
 
     def step(u, _):
         @pl.when(jnp.logical_and(u >= 2, u < 8))
@@ -371,21 +377,28 @@
                 ycopy(2, t).wait_recv()
                 zcopy(2, t).start()
 
-        @pl.when(u == 5)
+        for n, k in ((1, k_units[2]), (2, k_units[3]), (5, 2)):
+
+            @pl.when(u == n)
+            def _(k=k):
+                ecopy(k).wait_recv()
+                for t in range(2):
+                    ccopy(k, t).start()
+
+        @pl.when(u == HALO_UNIT)
         def _():
-            ecopy(2).wait_recv()
-            for t in range(2):
-                ccopy(2, t).start()
+            xz().wait_recv()
+            xc(1, zsp).start()
+            yzcopy().wait_recv()
+            yc(1, zsp, CORNERS).start()
 
         @pl.when(u >= 1)
         def _():
             k, t = unit(u - 1)
             b = before(k)
 
-            @pl.when(u >= 3)
-            def _():
-                ccopy(k, t).wait_recv()
-                cfcopy(k, t).wait_recv()
+            ccopy(k, t).wait_recv()
+            cfcopy(k, t).wait_recv()
 
             stage1(2 * b + t, [halo_cols(i, eight(b), t) for i in range(S)])
 
@@ -414,11 +427,12 @@
                 ycopy(k, t).wait_send()
         if k:
             ecopy(k).wait_send()
-            hcopy(k).wait_send()
+            hcopy(k, 0).wait_send()
+        hcopy(k, 1).wait_send()
     xz().wait_send()
     yzcopy().wait_send()
     for q in range(2):
-        for c in (xc(q, sp), yc(q, sp)):
+        for c in (xc(q, sp), yc(q, sp, COLUMNS), yc(q, sp, CORNERS)):
             c.wait_send()
     for side, cond in ((0, up), (1, down)):
 
@@ -448,7 +462,7 @@
             pltpu.VMEM((2, 1152, COLS), jnp.bfloat16),
             pltpu.VMEM((len(PAIRS), 8 * GROUP, 128), f32),
         ]
-        + [pltpu.SemaphoreType.DMA((n,)) for n in (8, 8, 4, 4, 8, 8, 16, 16, 10, 10, 16, 4, 2)],
+        + [pltpu.SemaphoreType.DMA((n,)) for n in (8, 8, 4, 4, 8, 8, 16, 16, 16, 16, 16, 4, 2)],
         name="correlate",
         compiler_params=pltpu.CompilerParams(
             collective_id=0, has_side_effects=True, vmem_limit_bytes=48 << 20

time: 37 us -> 36 us (0.973)
  Pallas kernels: 35 us -> 34 us
    pallas_call x1, Pallas kernels: 35 us -> 34 us  [shards(): pl.pallas_call(kernel, out_shape=jax.ShapeDtypeStruct((len(PAIRS), 2, ROW...]
where the time goes in v5:
time: 36 us; the launch traced here: 35.9 us
  Pallas kernels  34 us (94%)
  local copies, waits for them, and re-layouts  1.84 us (5%)
    pallas_call x1, Pallas kernels, shards(): pl.pallas_call(kernel, out_shape=jax.ShapeDtypeStruct((len(PAIRS), 2, ROW...  34 us
    unnamed x1, local copies, waits for them, and re-layouts  1.84 us

profile of v5, /device:TPU:1, one launch (start us, length us, event | category | flops | bytes accessed | tf_op | source)
XLA Modules:
  0.0 35.9 jit_solution(3059733661058730140)
XLA Ops:
  0.0 34.0 %correlate.1 = f32[28,2,64,256]{3,2,1,0:T(8,128)S(1)} custom-call(f32[2,8,16,1024]{3,2,1,0:T(8,128)} %x.1), custom_call_target="tpu_custom_call" | custom-call | tf_op jit(solution)/shard_map/correlate/pallas_call | solution.py:448
  34.0 1.8 %copy.3 = f32[28,2,64,256]{3,2,1,0:T(8,128)} copy(f32[28,2,64,256]{3,2,1,0:T(8,128)S(1)} %correlate.1) | data formatting | bytes 7340032

commit v6 on v5

--- a/solution.py
+++ b/solution.py
@@ -62,106 +62,6 @@
 
     load = pltpu.make_async_copy(x, xin, lsem.at[0])
     load.start()
-    pl.semaphore_wait(barrier, 8 + 4 * up.astype(jnp.int32) + 4 * down.astype(jnp.int32))
-
-    def rcopy(src, dst, ss, rs, dev):
-        return pltpu.make_async_remote_copy(
-            src_ref=src, dst_ref=dst, send_sem=ss, recv_sem=rs, device_id=dev, device_id_type=MESH
-        )
-
-    def cols(y):
-        return pl.ds(pl.multiple_of(y * COLS, COLS), COLS)
-
-    def tile_of(b, t):
-        return pl.ds(pl.multiple_of(b * BLK + 8 * t, 8), 8)
-
-    def pick(u, values):
-        return sum(v * (u == n).astype(jnp.int32) for n, v in enumerate(values))
-
-    t_sent, t_got = pick(ty, (0, 0, 1)), pick(ty, (1,))
-    turn = pick(ty, (1,))
-    k_units = (0, 0) + (1 + 2 * turn, 3 - 2 * turn) * 2 + (2, 2)
-    t_units = (0, 1, 1 - turn, turn, turn, 1 - turn, t_got, 1 - t_got)
-
-    def eight(b):
-        return pl.ds(pl.multiple_of(b * 8, 8), 8)
-
-    zdev = (zsp, tx, ty)
-    cdev = (csp, tx, ty)
-    mine = pl.ds(2 * sp, 2)
-    far = pl.ds(2 * zsp, 2)
-    six = pl.ds(p_here + 2, 6)
-    six_there = pl.ds(p_there + 2, 6)
-    own_rows = pl.ds(pl.multiple_of(ty * BLK, BLK), BLK)
-
-    def ycopy(k, t):
-        return rcopy(
-            x.at[:, pl.ds(p_there, 6), eight(t), cols(after(k))],
-            m.at[mine, six_there, tile_of(ty, t)],
-            ysend.at[2 * k + t], yrecv.at[2 * k + t], (sp, tx, after(k)),
-        )
-
-    def ecopy(k):
-        return rcopy(
-            x.at[:, pl.ds(p_extra, 2), :, cols(after(k))],
-            m.at[mine, pl.ds(p_extra + 2, 2), own_rows],
-            esend.at[k], erecv.at[k], (sp, tx, after(k)),
-        )
-
-    def zcopy(k, t, first=False):
-        dst = m.at[mine, six_there, tile_of(before(k), t)]
-        src = x.at[:, pl.ds(p_there, 6), 8 * t : 8 * t + 8, cols(ty)] if first else dst
-        return rcopy(src, dst, zsend.at[2 * k + t], zrecv.at[2 * k + t], zdev)
-
-    def ccopy(k, t, first=False):
-        dst = m.at[mine, six, tile_of(before(k), t)]
-        src = x.at[:, pl.ds(p_here, 6), 8 * t : 8 * t + 8, cols(ty)] if first else dst
-        return rcopy(src, dst, csend.at[2 * k + t], crecv.at[2 * k + t], cdev)
-
-    def cfcopy(k, t):
-        ref = m.at[far, six, tile_of(before(k), t)]
-        return rcopy(ref, ref, csend.at[8 + 2 * k + t], crecv.at[8 + 2 * k + t], cdev)
-
-    def hcopy(k, there):
-        dev = (zsp if there else sp, tx, after(k))
-        q = 4 * there + k
-        return rcopy(yhs.at[after(k)], yh.at[sp, eight(ty)], hsend.at[q], hrecv.at[q], dev)
-
-    def xcopies(side, y):
-        dev = (sp, tx + 1 if side == 0 else tx - 1, y)
-        q = 2 * (4 * side + y)
-        return (
-            rcopy(xhs.at[y], xb.at[sp, side], xsend.at[q], xrecv.at[2 * side], dev),
-            rcopy(
-                yhs.at[y], yh.at[sp, 32 + 8 * side : 40 + 8 * side],
-                xsend.at[q + 1], xrecv.at[2 * side + 1], dev,
-            ),
-        )
-
-    def xrows(first):
-        return pl.ds(pl.multiple_of(first * 4, 8), 24)
-
-    def xz():
-        ref = xb.at[sp, :, xrows(p_there)]
-        return rcopy(ref, ref, hsend.at[8], hrecv.at[8], zdev)
-
-    def yzcopy():
-        ref = yh.at[sp, CORNERS]
-        return rcopy(ref, ref, hsend.at[9], hrecv.at[9], zdev)
-
-    def xc(q, who):
-        ref = xb.at[who, :, xrows(p_here)]
-        return rcopy(ref, ref, hsend.at[10 + q], hrecv.at[10 + q], cdev)
-
-    def yc(q, who, part):
-        ref = yh.at[who, part]
-        q = q + (12 if part is COLUMNS else 14)
-        return rcopy(ref, ref, hsend.at[q], hrecv.at[q], cdev)
-
-    zcopy(0, 0, True).start()
-    for k, t in Y_ORDER[:2]:
-        ycopy(k, t).start()
-
     load.wait()
     row8 = lax.broadcasted_iota(jnp.int32, (8, 128), 0)
     lane8 = lax.broadcasted_iota(jnp.int32, (8, 128), 1)
@@ -183,12 +83,6 @@
                     acc = jnp.where(jnp.logical_and(lane8 >= base + 2, lane8 < base + 4), left, acc)
         yhs[y] = acc
 
-    yh[sp, eight(ty)] = yhs[ty]
-    for k in (2, 1, 3):
-        hcopy(k, 1).start()
-        hcopy(k, 0).start()
-    hcopy(0, 1).start()
-
     def pack_rows(first):
         for y in range(4):
             for z in range(NZ):
@@ -196,23 +90,129 @@
                     r = 4 * z + 2 * s
                     xhs[y, r : r + 2, :] = xin[s, z, first : first + 2, y * COLS : (y + 1) * COLS]
 
+    for cond, first in ((up, 14), (down, 0)):
+
+        @pl.when(cond)
+        def _(first=first):
+            pack_rows(first)
+
+    pl.semaphore_wait(barrier, 8 + 4 * up.astype(jnp.int32) + 4 * down.astype(jnp.int32))
+
+    def rcopy(src, dst, ss, rs, dev):
+        return pltpu.make_async_remote_copy(
+            src_ref=src, dst_ref=dst, send_sem=ss, recv_sem=rs, device_id=dev, device_id_type=MESH
+        )
+
+    def cols(y):
+        return pl.ds(pl.multiple_of(y * COLS, COLS), COLS)
+
+    def tile_of(b, t):
+        return pl.ds(pl.multiple_of(b * BLK + 8 * t, 8), 8)
+
+    def pick(u, values):
+        return sum(v * (u == n).astype(jnp.int32) for n, v in enumerate(values))
+
+    t_sent, t_got = pick(ty, (0, 0, 1)), pick(ty, (1,))
+    turn = pick(ty, (1,))
+    k_units = (0, 0) + (1 + 2 * turn, 3 - 2 * turn) * 2 + (2, 2)
+    t_units = (0, 1, 1 - turn, turn, turn, 1 - turn, t_got, 1 - t_got)
+
+    def eight(b):
+        return pl.ds(pl.multiple_of(b * 8, 8), 8)
+
+    zdev = (zsp, tx, ty)
+    cdev = (csp, tx, ty)
+    mine = pl.ds(2 * sp, 2)
+    far = pl.ds(2 * zsp, 2)
+    six = pl.ds(p_here + 2, 6)
+    six_there = pl.ds(p_there + 2, 6)
+    own_rows = pl.ds(pl.multiple_of(ty * BLK, BLK), BLK)
+
+    def ycopy(k, t):
+        return rcopy(
+            x.at[:, pl.ds(p_there, 6), eight(t), cols(after(k))],
+            m.at[mine, six_there, tile_of(ty, t)],
+            ysend.at[2 * k + t], yrecv.at[2 * k + t], (sp, tx, after(k)),
+        )
+
+    def ecopy(k):
+        return rcopy(
+            x.at[:, pl.ds(p_extra, 2), :, cols(after(k))],
+            m.at[mine, pl.ds(p_extra + 2, 2), own_rows],
+            esend.at[k], erecv.at[k], (sp, tx, after(k)),
+        )
+
+    def zcopy(k, t, first=False):
+        dst = m.at[mine, six_there, tile_of(before(k), t)]
+        src = x.at[:, pl.ds(p_there, 6), 8 * t : 8 * t + 8, cols(ty)] if first else dst
+        return rcopy(src, dst, zsend.at[2 * k + t], zrecv.at[2 * k + t], zdev)
+
+    def ccopy(k, t, first=False):
+        dst = m.at[mine, six, tile_of(before(k), t)]
+        src = x.at[:, pl.ds(p_here, 6), 8 * t : 8 * t + 8, cols(ty)] if first else dst
+        return rcopy(src, dst, csend.at[2 * k + t], crecv.at[2 * k + t], cdev)
+
+    def cfcopy(k, t):
+        ref = m.at[far, six, tile_of(before(k), t)]
+        return rcopy(ref, ref, csend.at[8 + 2 * k + t], crecv.at[8 + 2 * k + t], cdev)
+
+    def hcopy(k, there):
+        dev = (zsp if there else sp, tx, after(k))
+        q = 4 * there + k
+        return rcopy(yhs.at[after(k)], yh.at[sp, eight(ty)], hsend.at[q], hrecv.at[q], dev)
+
+    def xcopies(side, y):
+        dev = (sp, tx + 1 if side == 0 else tx - 1, y)
+        q = 2 * (4 * side + y)
+        return (
+            rcopy(xhs.at[y], xb.at[sp, side], xsend.at[q], xrecv.at[2 * side], dev),
+            rcopy(
+                yhs.at[y], yh.at[sp, 32 + 8 * side : 40 + 8 * side],
+                xsend.at[q + 1], xrecv.at[2 * side + 1], dev,
+            ),
+        )
+
+    def xrows(first):
+        return pl.ds(pl.multiple_of(first * 4, 8), 24)
+
+    def xz():
+        ref = xb.at[sp, :, xrows(p_there)]
+        return rcopy(ref, ref, hsend.at[8], hrecv.at[8], zdev)
+
+    def yzcopy():
+        ref = yh.at[sp, CORNERS]
+        return rcopy(ref, ref, hsend.at[9], hrecv.at[9], zdev)
+
+    def xc(q, who):
+        ref = xb.at[who, :, xrows(p_here)]
+        return rcopy(ref, ref, hsend.at[10 + q], hrecv.at[10 + q], cdev)
+
+    def yc(q, who, part):
+        ref = yh.at[who, part]
+        q = q + (12 if part is COLUMNS else 14)
+        return rcopy(ref, ref, hsend.at[q], hrecv.at[q], cdev)
+
+    zcopy(0, 0, True).start()
     for side, cond, first in ((0, up, 14), (1, down, 0)):
 
         @pl.when(cond)
         def _(side=side, first=first):
-            pack_rows(first)
             for y in range(4):
                 for c in xcopies(side, y):
                     c.start()
 
+    yh[sp, eight(ty)] = yhs[ty]
+    for k in (2, 1, 3):
+        hcopy(k, 1).start()
+        hcopy(k, 0).start()
+    hcopy(0, 1).start()
+
+    for k, t in Y_ORDER[:2]:
+        ycopy(k, t).start()
+
     zcopy(0, 1, True).start()
     for k, t in Y_ORDER[2:]:
         ycopy(k, t).start()
-    ecopy(1).start()
-    ecopy(3).start()
-    ycopy(2, t_sent).start()
-    ycopy(2, 1 - t_sent).start()
-    ecopy(2).start()
     for t in range(2):
         ccopy(0, t, True).start()
     own = pltpu.make_async_copy(
@@ -234,6 +234,12 @@
     for k, t in list(zip(k_units, t_units))[2:4]:
         ycopy(k, t).wait_recv()
         zcopy(k, t).start()
+    ecopy(1).start()
+    ecopy(3).start()
+    ycopy(2, t_sent).start()
+    ycopy(2, 1 - t_sent).start()
+    ecopy(2).start()
+
     for k in range(4):
         hcopy(k, 1).wait_recv()
         if k:

time: 36 us -> 35.1 us (0.975)
  Pallas kernels: 34 us -> 32.9 us
    pallas_call x1, Pallas kernels: 34 us -> 32.9 us  [shards(): pl.pallas_call(kernel, out_shape=jax.ShapeDtypeStruct((len(PAIRS), 2, ROW...]
where the time goes in v6:
time: 35.1 us; the launch traced here: 34.7 us
  Pallas kernels  32.9 us (94%)
  local copies, waits for them, and re-layouts  1.84 us (5%)
    pallas_call x1, Pallas kernels, shards(): pl.pallas_call(kernel, out_shape=jax.ShapeDtypeStruct((len(PAIRS), 2, ROW...  32.9 us
    unnamed x1, local copies, waits for them, and re-layouts  1.84 us

profile of v6, /device:TPU:1, one launch (start us, length us, event | category | flops | bytes accessed | tf_op | source)
XLA Modules:
  0.0 34.7 jit_solution(13641524434959376727)
XLA Ops:
  0.0 32.9 %correlate.1 = f32[28,2,64,256]{3,2,1,0:T(8,128)S(1)} custom-call(f32[2,8,16,1024]{3,2,1,0:T(8,128)} %x.1), custom_call_target="tpu_custom_call" | custom-call | tf_op jit(solution)/shard_map/correlate/pallas_call | solution.py:454
  32.9 1.8 %copy.3 = f32[28,2,64,256]{3,2,1,0:T(8,128)} copy(f32[28,2,64,256]{3,2,1,0:T(8,128)S(1)} %correlate.1) | data formatting | bytes 7340032

commit v7 on v6

--- a/solution.py
+++ b/solution.py
@@ -155,6 +155,14 @@
     def cfcopy(k, t):
         ref = m.at[far, six, tile_of(before(k), t)]
         return rcopy(ref, ref, csend.at[8 + 2 * k + t], crecv.at[8 + 2 * k + t], cdev)
+
+    def zlast(s):
+        ref = m.at[2 * sp + s, six_there, tile_of(before(2), 1 - t_got)]
+        return rcopy(ref, ref, zsend.at[8 + s], zrecv.at[8 + s], zdev)
+
+    def cflast(s):
+        ref = m.at[2 * zsp + s, six, tile_of(before(2), 1 - t_got)]
+        return rcopy(ref, ref, csend.at[16 + s], crecv.at[16 + s], cdev)
 
     def hcopy(k, there):
         dev = (zsp if there else sp, tx, after(k))
@@ -370,18 +378,28 @@
         return pick(u, k_units), pick(u, t_units)
 
     def step(u, _):
-        @pl.when(jnp.logical_and(u >= 2, u < 8))
+        @pl.when(jnp.logical_and(u >= 2, u < 7))
         def _():
             k, t = unit(u)
             zcopy(k, t).wait_recv()
             cfcopy(k, t).start()
 
-        for n, t in ((3, t_got), (4, 1 - t_got)):
-
-            @pl.when(u == n)
-            def _(t=t):
-                ycopy(2, t).wait_recv()
-                zcopy(2, t).start()
+        @pl.when(u == 7)
+        def _():
+            for s in range(2):
+                zlast(s).wait_recv()
+                cflast(s).start()
+
+        @pl.when(u == 3)
+        def _():
+            ycopy(2, t_got).wait_recv()
+            zcopy(2, t_got).start()
+
+        @pl.when(u == 4)
+        def _():
+            ycopy(2, 1 - t_got).wait_recv()
+            for s in range(2):
+                zlast(s).start()
 
         for n, k in ((1, k_units[2]), (2, k_units[3]), (5, 2)):
 
@@ -404,7 +422,15 @@
             b = before(k)
 
             ccopy(k, t).wait_recv()
-            cfcopy(k, t).wait_recv()
+
+            @pl.when(u < 8)
+            def _():
+                cfcopy(k, t).wait_recv()
+
+            @pl.when(u == 8)
+            def _():
+                for s in range(2):
+                    cflast(s).wait_recv()
 
             stage1(2 * b + t, [halo_cols(i, eight(b), t) for i in range(S)])
 
@@ -426,15 +452,21 @@
 
     for k in range(4):
         for t in range(2):
-            zcopy(k, t).wait_send()
+            if k != 2:
+                zcopy(k, t).wait_send()
+                cfcopy(k, t).wait_send()
             ccopy(k, t).wait_send()
-            cfcopy(k, t).wait_send()
             if k:
                 ycopy(k, t).wait_send()
         if k:
             ecopy(k).wait_send()
             hcopy(k, 0).wait_send()
         hcopy(k, 1).wait_send()
+    zcopy(2, t_got).wait_send()
+    cfcopy(2, t_got).wait_send()
+    for s in range(2):
+        zlast(s).wait_send()
+        cflast(s).wait_send()
     xz().wait_send()
     yzcopy().wait_send()
     for q in range(2):
@@ -468,7 +500,7 @@
             pltpu.VMEM((2, 1152, COLS), jnp.bfloat16),
             pltpu.VMEM((len(PAIRS), 8 * GROUP, 128), f32),
         ]
-        + [pltpu.SemaphoreType.DMA((n,)) for n in (8, 8, 4, 4, 8, 8, 16, 16, 16, 16, 16, 4, 2)],
+        + [pltpu.SemaphoreType.DMA((n,)) for n in (8, 8, 4, 4, 10, 10, 18, 18, 16, 16, 16, 4, 2)],
         name="correlate",
         compiler_params=pltpu.CompilerParams(
             collective_id=0, has_side_effects=True, vmem_limit_bytes=48 << 20

time: 35.1 us -> 35.3 us (level)
  no operation moved by 1% of the time
where the time goes in v7:
time: 35.3 us; the launch traced here: 34.9 us
  Pallas kernels  33 us (93%)
  local copies, waits for them, and re-layouts  1.84 us (5%)
    pallas_call x1, Pallas kernels, shards(): pl.pallas_call(kernel, out_shape=jax.ShapeDtypeStruct((len(PAIRS), 2, ROW...  33 us
    unnamed x1, local copies, waits for them, and re-layouts  1.84 us

profile of v7, /device:TPU:1, one launch (start us, length us, event | category | flops | bytes accessed | tf_op | source)
XLA Modules:
  0.0 34.9 jit_solution(8490765896922339533)
XLA Ops:
  0.0 33.0 %correlate.1 = f32[28,2,64,256]{3,2,1,0:T(8,128)S(1)} custom-call(f32[2,8,16,1024]{3,2,1,0:T(8,128)} %x.1), custom_call_target="tpu_custom_call" | custom-call | tf_op jit(solution)/shard_map/correlate/pallas_call | solution.py:486
  33.1 1.8 %copy.3 = f32[28,2,64,256]{3,2,1,0:T(8,128)} copy(f32[28,2,64,256]{3,2,1,0:T(8,128)S(1)} %correlate.1) | data formatting | bytes 7340032
